TPU v7x, 32 devices: a whole 2x2x4 slice. The times are simulated.
32 devices in a mesh: comp: 2 (over y), ty: 4 (over z), tx: 4 (over x, core).
Axes of the slice: x: 2, y: 2, z: 4, core: 2. Of those that a mesh axis runs over, the one named last changes fastest.
Arguments:
- atm_flux: float32 [8, 524288], P(None, ('comp', 'ty', 'tx')), may hold values from -6 to 6
- margin_source: int32 [8192, 128], P(('comp', 'ty', 'tx')), may hold values from 0 to 127
- margin_cell: int32 [8192, 128], P(('comp', 'ty', 'tx')), may hold values from 0 to 65535, as said below
- margin_weight: float32 [8192, 128], P(('comp', 'ty', 'tx')), may hold values from 0 to 1
- margin_tile: int32 [8192, 1], P(('comp', 'ty', 'tx')), may hold values from 0 to 31; in each aligned block of 256 rows (0 to 255, 256 to 511, ...) at most 16 rows name the same one
- land_mask: int32 [512, 4096], P(('comp', 'ty'), 'tx'), may hold values 0 or 1
- sea_depth: float32 [512, 4096], P(('comp', 'ty'), 'tx'), may hold values from 0.5 to 1.8
- sea_height: float32 [512, 4096], P(('comp', 'ty'), 'tx'), may hold values from -3 to 3
- transport: float32 [2, 512, 4096], P(None, ('comp', 'ty'), 'tx'), may hold values from -3 to 3
- tracers: float32 [2, 16, 512, 4096], P(None, None, ('comp', 'ty'), 'tx'), may hold values from -6 to 6
Outputs:
- new_height: float32 [512, 4096], P(('comp', 'ty'), 'tx')
- new_transport: float32 [2, 512, 4096], P(None, ('comp', 'ty'), 'tx')
- new_tracers: float32 [2, 16, 512, 4096], P(None, None, ('comp', 'ty'), 'tx')
Inputs may be any that keep to these rules, and one draw needn't show every extreme that they name: `margin_tile`: among the 256 blocks of one atmosphere owner (an aligned run of 256 rows), no ocean tile is named by more than 16 blocks. All entries of one block lie in one row of its tile: margin_cell[b, j] // 1024 is the same for every j.
All inputs are finite; a program needn't handle non-finite values. No bound on the sum of `land_mask` on one device may be relied on, other than what follows from the above.
Results may differ from a plain program's by a relative error of at most 0.000088.
Values sent between devices are 32-bit elements; how exact they have to be, the bound alone decides.
A program may use at most 192 MiB of HBM per device.

v0:
```python
import functools

import jax
import jax.numpy as jnp
import numpy as np
from jax import lax
from jax.experimental import pallas as pl
from jax.experimental.pallas import tpu as pltpu
from jax.sharding import PartitionSpec as P

SUB = 3
RIM = 8
LANES = 128
AXES = ("comp", "ty", "tx")

damping = 0.95
advect = 0.15
diffuse = 0.1

f32 = jnp.float32
VMEM_LIMIT = 56 * 1024 * 1024


def vmem():
    return pl.BlockSpec(memory_space=pltpu.VMEM)


def smem():
    return pl.BlockSpec(memory_space=pltpu.SMEM)


def pack_kernel(cap, tile_ref, flux_ref, src_ref, cell_ref, weight_ref, out_ref, count_ref):
    tiles = out_ref.shape[0]
    blocks = src_ref.shape[0]
    fields = flux_ref.shape[0]
    width = src_ref.shape[1]

    def clear(t, carry):
        out_ref[t] = jnp.zeros(out_ref.shape[1:], f32)
        count_ref[t] = 0
        return carry

    lax.fori_loop(0, tiles, clear, 0)

    def group(g, carry):
        base = pl.multiple_of(g * 8, 8)
        sources = src_ref[pl.ds(base, 8), :]
        cells = cell_ref[pl.ds(base, 8), :].astype(f32)
        weights = weight_ref[pl.ds(base, 8), :]
        for w in range(4):
            start = pl.multiple_of((g * 4 + w) * width, width)
            window = flux_ref[:, pl.ds(start, width)]
            for half in range(2):
                j = 2 * w + half
                index = jnp.broadcast_to(sources[j : j + 1], (fields, width))
                picked = jnp.take_along_axis(window, index, axis=1)
                t = tile_ref[base + j]
                r = count_ref[t]
                count_ref[t] = r + 1
                at = pl.multiple_of(r * fields, fields)
                out_ref[t, pl.ds(at, fields), :] = picked * weights[j : j + 1]
                out_ref[t, pl.ds(cap * fields + r, 1), :] = cells[j : j + 1]
        return carry

    lax.fori_loop(0, blocks // 8, group, 0)


def pack(margin_tile, atm_flux, margin_source, margin_cell, margin_weight, tiles, cap):
    fields = atm_flux.shape[0]
    rows = cap * fields + -(-cap // 8) * 8
    return pl.pallas_call(
        functools.partial(pack_kernel, cap),
        out_shape=jax.ShapeDtypeStruct((tiles, rows, margin_source.shape[1]), f32),
        in_specs=[smem(), vmem(), vmem(), vmem(), vmem()],
        out_specs=vmem(),
        scratch_shapes=[pltpu.SMEM((tiles,), jnp.int32)],
        compiler_params=pltpu.CompilerParams(vmem_limit_bytes=VMEM_LIMIT),
        cost_estimate=pl.CostEstimate(flops=10_000_000, bytes_accessed=4_000_000, transcendentals=0),
        name="pack",
    )(margin_tile, atm_flux, margin_source, margin_cell, margin_weight)


def scatter_kernel(cap, fields, row_ref, in_ref, forcing_ref, baro_ref, acc_ref):
    owners = in_ref.shape[0]
    width = in_ref.shape[2]
    tile_rows, tile_cols = forcing_ref.shape[1:]
    highs = tile_cols // LANES
    lines = highs * fields
    group = 4 if cap % 4 == 0 else 1

    def clear(y, carry):
        acc_ref[pl.ds(pl.multiple_of(y * lines, lines), lines), :] = jnp.zeros((lines, LANES), f32)
        return carry

    lax.fori_loop(0, tile_rows, clear, 0)
    low_iota = lax.broadcasted_iota(jnp.int32, (LANES, width), 0)

    def owner_step(o, carry):
        cells = in_ref[o, cap * fields : in_ref.shape[1], :].astype(jnp.int32)
        for g in range(cap // group):
            sums = []
            for r in range(g * group, (g + 1) * group):
                row = row_ref[o * cap + r]
                cols = cells[r : r + 1] - row * tile_cols
                high = jnp.broadcast_to(cols // LANES, (fields, width))
                low = jnp.broadcast_to(cols % LANES, (LANES, width))
                onehot = jnp.where(low_iota == low, 1.0, 0.0).astype(jnp.bfloat16)
                values = in_ref[o, r * fields : (r + 1) * fields, :]
                coarse = values.astype(jnp.bfloat16).astype(f32)
                fine = values - coarse
                picks = [high == h for h in range(highs)]
                left = jnp.concatenate(
                    [jnp.where(p, coarse, 0.0) for p in picks]
                    + [jnp.where(p, fine, 0.0) for p in picks],
                    axis=0,
                ).astype(jnp.bfloat16)
                both = lax.dot_general(
                    left, onehot, (((1,), (1,)), ((), ())), preferred_element_type=f32
                )
                sums.append((row, both[:lines] + both[lines:]))
            for row, part in sums:
                at = pl.ds(pl.multiple_of(row * lines, lines), lines)
                acc_ref[at, :] = acc_ref[at, :] + part
        return carry

    lax.fori_loop(0, owners, owner_step, 0)

    def unfold(yb, carry):
        ys = pl.ds(pl.multiple_of(yb * 8, 8), 8)
        for h in range(highs):
            cs = slice(h * LANES, (h + 1) * LANES)
            planes = []
            for f in range(fields):
                part = acc_ref[pl.ds(yb * 8 * lines + h * fields + f, 8, stride=lines), :]
                forcing_ref[f, ys, cs] = part
                planes.append(part)
            baro_ref[0, ys, cs] = 0.5 * planes[2]
            baro_ref[1, ys, cs] = 0.5 * planes[0]
            baro_ref[2, ys, cs] = 0.5 * planes[1]
            baro_ref[3, ys, cs] = 0.1 * (planes[6] - planes[5])
        return carry

    lax.fori_loop(0, tile_rows // 8, unfold, 0)


def scatter(rows, arrived, cap, fields, tile_rows, tile_cols):
    lines = tile_cols // LANES * fields
    return pl.pallas_call(
        functools.partial(scatter_kernel, cap, fields),
        out_shape=(
            jax.ShapeDtypeStruct((fields, tile_rows, tile_cols), f32),
            jax.ShapeDtypeStruct((4, tile_rows, tile_cols), f32),
        ),
        in_specs=[smem(), vmem()],
        out_specs=(vmem(), vmem()),
        scratch_shapes=[pltpu.VMEM((tile_rows * lines, LANES), f32)],
        compiler_params=pltpu.CompilerParams(vmem_limit_bytes=VMEM_LIMIT),
        cost_estimate=pl.CostEstimate(
            flops=2_000_000_000, bytes_accessed=5_000_000, transcendentals=0
        ),
        name="scatter",
    )(rows, arrived)


def edges_kernel(west_ref, east_ref, mask_west_ref, mask_east_ref, first_ref, last_ref):
    planes, rows = west_ref.shape[:2]
    lane = lax.broadcasted_iota(jnp.int32, (rows, LANES), 1)
    for src, mask, dst, col in (
        (west_ref, mask_west_ref, first_ref, 0),
        (east_ref, mask_east_ref, last_ref, LANES - 1),
    ):
        total = jnp.zeros((rows, LANES), f32)
        for p in range(planes):
            total = jnp.where(
                lane == p, jnp.broadcast_to(src[p, :, col : col + 1], (rows, LANES)), total
            )
        edge = mask[:, col : col + 1].astype(f32)
        dst[...] = jnp.where(lane == planes, jnp.broadcast_to(edge, (rows, LANES)), total)


def edge_columns(tracers, land_mask):
    planes, rows, cols = tracers.shape
    end = cols // LANES - 1
    strip = jax.ShapeDtypeStruct((rows, LANES), f32)
    whole = pl.BlockSpec((rows, LANES), lambda i: (0, 0))
    return pl.pallas_call(
        edges_kernel,
        out_shape=(strip, strip),
        grid=(1,),
        in_specs=[
            pl.BlockSpec((planes, rows, LANES), lambda i: (0, 0, 0)),
            pl.BlockSpec((planes, rows, LANES), lambda i: (0, 0, end)),
            pl.BlockSpec((rows, LANES), lambda i: (0, 0)),
            pl.BlockSpec((rows, LANES), lambda i: (0, end)),
        ],
        out_specs=(whole, whole),
        compiler_params=pltpu.CompilerParams(vmem_limit_bytes=VMEM_LIMIT),
        name="edges",
    )(tracers, tracers, land_mask, land_mask)


def tracer_kernel(
    levels,
    tracer_hbm,
    south_ref,
    north_ref,
    west_ref,
    east_ref,
    mask_south_ref,
    mask_north_ref,
    mask_ref,
    depth_ref,
    flow_ref,
    forcing_ref,
    out_ref,
    held,
    mask_held,
    ratio_ref,
    sems,
):
    planes = held.shape[0]
    rows, cols = mask_ref.shape
    steps = rows // 8
    i = pl.program_id(0)

    def chunk(step):
        at = pl.multiple_of(step * 8, 8)
        return pltpu.make_async_copy(
            tracer_hbm.at[:, pl.ds(at, 8), :], held.at[:, pl.ds(at + 8, 8), :], sems.at[step]
        )

    @pl.when(i == 0)
    def _():
        for s in range(steps):
            chunk(s).start()
        for p in range(planes):
            held[p, 7:8, :] = south_ref[p : p + 1, :]
            held[p, rows + 8 : rows + 9, :] = north_ref[p : p + 1, :]
        mask_held[0:8, :] = mask_south_ref[...]
        mask_held[8 : rows + 8, :] = mask_ref[...].astype(f32)
        mask_held[rows + 8 : rows + 16, :] = mask_north_ref[...]
        chunk(0).wait()

    @pl.when(i < steps - 1)
    def _():
        chunk(i + 1).wait()

    base = pl.multiple_of(i * 8, 8)
    here = pl.ds(base + 8, 8)
    lane = lax.broadcasted_iota(jnp.int32, (8, cols), 1) % LANES
    sub = lax.broadcasted_iota(jnp.int32, (8, cols), 0)
    at_first, at_last = lane == 0, lane == LANES - 1
    at_bottom, at_top = sub == 0, sub == 7
    west_edges = west_ref[pl.ds(base, 8), :]
    east_edges = east_ref[pl.ds(base, 8), :]
    pieces = cols // LANES

    def sides(q, below, above, p):
        parts = [q[:, c * LANES : (c + 1) * LANES] for c in range(pieces)]
        up = [pltpu.roll(a, 1, 1) for a in parts]
        down = [pltpu.roll(a, LANES - 1, 1) for a in parts]
        west_edge = jnp.broadcast_to(west_edges[:, p : p + 1], (8, LANES))
        east_edge = jnp.broadcast_to(east_edges[:, p : p + 1], (8, LANES))
        west = jnp.where(
            at_first, jnp.concatenate([west_edge] + up[:-1], 1), jnp.concatenate(up, 1)
        )
        east = jnp.where(
            at_last, jnp.concatenate(down[1:] + [east_edge], 1), jnp.concatenate(down, 1)
        )
        south = jnp.where(at_bottom, jnp.broadcast_to(below, q.shape), pltpu.roll(q, 1, 0))
        north = jnp.where(at_top, jnp.broadcast_to(above, q.shape), pltpu.roll(q, 7, 0))
        return east, west, north, south

    mask = mask_held[here, :]
    mask_e, mask_w, mask_n, mask_s = sides(
        mask, mask_held[pl.ds(base + 7, 1), :], mask_held[pl.ds(base + 16, 1), :], planes
    )
    inverse = 1.0 / depth_ref[...]
    u = flow_ref[0] * inverse
    v = flow_ref[1] * inverse
    ce = mask_e * (diffuse - advect * jnp.minimum(u, 0.0))
    cw = mask_w * (diffuse + advect * jnp.maximum(u, 0.0))
    cn = mask_n * (diffuse - advect * jnp.minimum(v, 0.0))
    cs = mask_s * (diffuse + advect * jnp.maximum(v, 0.0))
    c0 = 1.0 - (ce + cw + cn + cs)

    depths = np.arange(levels, dtype=np.float32)
    absorb = np.exp(-depths / np.float32(3)) - np.exp(-(depths + 1) / np.float32(3))
    fade = np.exp(-depths / np.float32(2))
    stir = 0.5 * forcing_ref[7] * forcing_ref[7]
    sun = 0.5 * forcing_ref[4]
    ratio = None
    last = [None, None]
    lower = None
    for k in range(levels):
        upper = 0.2 + stir * float(fade[k]) if k < levels - 1 else None
        pivot = 1.0
        if upper is not None:
            pivot = pivot + upper
        if lower is not None:
            pivot = pivot + lower + lower * ratio
        scale = 1.0 / pivot
        if upper is not None:
            ratio = -upper * scale
            ratio_ref[k] = ratio
        for t in range(2):
            p = t * levels + k
            q = held[p, here, :]
            qe, qw, qn, qs = sides(
                q, held[p, pl.ds(base + 7, 1), :], held[p, pl.ds(base + 16, 1), :], p
            )
            side = c0 * q + ce * qe + cw * qw + cn * qn + cs * qs
            if t == 0:
                side = side + sun * float(absorb[k])
                if k == 0:
                    side = side + 0.5 * forcing_ref[3]
            elif k == 0:
                side = side + (0.5 * forcing_ref[5] - 0.3 * forcing_ref[6])
            if lower is not None:
                side = side + lower * last[t]
            last[t] = side * scale
            out_ref[p] = last[t]
        lower = upper
    ocean = mask > 0.5
    for k in range(levels - 1, -1, -1):
        for t in range(2):
            p = t * levels + k
            if k < levels - 1:
                last[t] = out_ref[p] - ratio_ref[k] * last[t]
            out_ref[p] = jnp.where(ocean, last[t], held[p, here, :])


def tracer_step(
    levels, tracers, south, north, west, east, mask_south, mask_north, mask, depth, flow, forcing
):
    planes, rows, cols = tracers.shape

    def band(*lead):
        zeros = (0,) * len(lead)
        return pl.BlockSpec((*lead, 8, cols), lambda i: (*zeros, i, 0))

    def full(a):
        zeros = (0,) * a.ndim
        return pl.BlockSpec(a.shape, lambda i: zeros)

    return pl.pallas_call(
        functools.partial(tracer_kernel, levels),
        out_shape=jax.ShapeDtypeStruct(tracers.shape, f32),
        grid=(rows // 8,),
        in_specs=[
            pl.BlockSpec(memory_space=pl.ANY),
            full(south),
            full(north),
            full(west),
            full(east),
            full(mask_south),
            full(mask_north),
            full(mask),
            band(),
            band(2),
            band(forcing.shape[0]),
        ],
        out_specs=band(planes),
        scratch_shapes=[
            pltpu.VMEM((planes, rows + 16, cols), f32),
            pltpu.VMEM((rows + 16, cols), f32),
            pltpu.VMEM((levels, 8, cols), f32),
            pltpu.SemaphoreType.DMA((rows // 8,)),
        ],
        compiler_params=pltpu.CompilerParams(
            vmem_limit_bytes=VMEM_LIMIT, dimension_semantics=("arbitrary",)
        ),
        cost_estimate=pl.CostEstimate(
            flops=100_000_000, bytes_accessed=40_000_000, transcendentals=0
        ),
        name="tracer",
    )(tracers, south, north, west, east, mask_south, mask_north, mask, depth, flow, forcing)


def baro_kernel(
    height_ref,
    flow_ref,
    mask_ref,
    depth_ref,
    baro_ref,
    south_ref,
    north_ref,
    west_ref,
    east_ref,
    fs_ref,
    fn_ref,
    fw_ref,
    fe_ref,
    fsw_ref,
    fse_ref,
    fnw_ref,
    fne_ref,
    height_out,
    flow_out,
):
    rows, cols = height_ref.shape

    def still(k, tile):
        middle = jnp.concatenate([south_ref[k], tile, north_ref[k]], 0)
        return jnp.concatenate([west_ref[k], middle, east_ref[k]], 1)

    def forced(k):
        low = jnp.concatenate([fsw_ref[k], fs_ref[k], fse_ref[k]], 1)
        mid = jnp.concatenate([fw_ref[k], baro_ref[k], fe_ref[k]], 1)
        top = jnp.concatenate([fnw_ref[k], fn_ref[k], fne_ref[k]], 1)
        return jnp.concatenate([low, mid, top], 0)

    height = still(0, height_ref[...])
    along = still(1, flow_ref[0])
    across = still(2, flow_ref[1])
    mask = still(3, mask_ref[...].astype(f32))
    bottom = -0.5 * still(4, depth_ref[...])
    pressure, wind_x, wind_y, source = [forced(k) for k in range(4)]
    tall, wide = height.shape

    def slope_x(a):
        return pltpu.roll(a, wide - 1, 1) - pltpu.roll(a, 1, 1)

    def slope_y(a):
        return pltpu.roll(a, tall - 1, 0) - pltpu.roll(a, 1, 0)

    for _ in range(SUB):
        level = mask * (height + pressure)
        along = mask * (damping * along + (bottom * slope_x(level) + wind_x))
        across = mask * (damping * across + (bottom * slope_y(level) + wind_y))
        height = mask * (height - 0.5 * (slope_x(along) + slope_y(across)) + source)
    inner = (slice(RIM, RIM + rows), slice(LANES, LANES + cols))
    height_out[...] = height[inner]
    flow_out[0] = along[inner]
    flow_out[1] = across[inner]


def local(
    ny,
    nx,
    atm_flux,
    margin_source,
    margin_cell,
    margin_weight,
    margin_tile,
    land_mask,
    sea_depth,
    sea_height,
    transport,
    tracers,
):
    levels = tracers.shape[1]
    tile_rows, tile_cols = sea_height.shape
    fields = atm_flux.shape[0]
    tiles = ny * nx
    cap = 2 * margin_source.shape[0] // tiles

    def from_side(a, dy, dx):
        perm = [
            ((y + dy) * nx + x + dx, y * nx + x)
            for y in range(ny)
            for x in range(nx)
            if 0 <= y + dy < ny and 0 <= x + dx < nx
        ]
        return lax.ppermute(a, AXES, perm)

    flat = tracers.reshape(2 * levels, tile_rows, tile_cols)
    still = jnp.stack(
        [sea_height, transport[0], transport[1], land_mask.astype(f32), sea_depth]
    )
    count = still.shape[0]

    def lines(edge, band):
        return jnp.concatenate([edge, band.reshape(count * RIM, tile_cols)], 0)

    planes = 2 * levels
    got_s = from_side(lines(flat[:, -1], still[:, -RIM:]), -1, 0)
    got_n = from_side(lines(flat[:, 0], still[:, :RIM]), 1, 0)
    still_s = got_s[planes:].reshape(count, RIM, tile_cols)
    still_n = got_n[planes:].reshape(count, RIM, tile_cols)
    tall = jnp.concatenate([still_s, still, still_n], 1)
    first, last = edge_columns(flat, land_mask)
    ext = (tile_rows + 2 * RIM) * count

    def columns(edge, band):
        return jnp.concatenate([edge, band.reshape(ext, LANES)], 0)

    got_w = from_side(columns(last, tall[:, :, -LANES:]), 0, -1)
    got_e = from_side(columns(first, tall[:, :, :LANES]), 0, 1)
    still_w = got_w[tile_rows:].reshape(count, -1, LANES)
    still_e = got_e[tile_rows:].reshape(count, -1, LANES)

    outgoing = pack(
        margin_tile[:, 0], atm_flux, margin_source, margin_cell, margin_weight, tiles, cap
    )
    arrived = lax.all_to_all(outgoing, AXES, split_axis=0, concat_axis=0, tiled=True)
    slot_rows = arrived[:, cap * fields : cap * fields + cap, 0].astype(jnp.int32) // tile_cols
    forcing, baro = scatter(
        slot_rows.reshape(-1), arrived, cap, fields, tile_rows, tile_cols
    )

    low, high = slice(None, RIM), slice(-RIM, None)
    left, right = slice(None, LANES), slice(-LANES, None)
    halo = [
        from_side(baro[:, high], -1, 0),
        from_side(baro[:, low], 1, 0),
        from_side(baro[:, :, right], 0, -1),
        from_side(baro[:, :, left], 0, 1),
        from_side(baro[:, high, right], -1, -1),
        from_side(baro[:, high, left], -1, 1),
        from_side(baro[:, low, right], 1, -1),
        from_side(baro[:, low, left], 1, 1),
    ]
    new_tracers = tracer_step(
        levels,
        flat,
        got_s[:planes],
        got_n[:planes],
        got_w[:tile_rows],
        got_e[:tile_rows],
        still_s[3],
        still_n[3],
        land_mask,
        sea_depth,
        transport,
        forcing,
    )
    height, flow = pl.pallas_call(
        baro_kernel,
        out_shape=(
            jax.ShapeDtypeStruct(sea_height.shape, f32),
            jax.ShapeDtypeStruct(transport.shape, f32),
        ),
        in_specs=[vmem()] * 17,
        out_specs=(vmem(), vmem()),
        compiler_params=pltpu.CompilerParams(vmem_limit_bytes=VMEM_LIMIT),
        name="baro",
    )(
        sea_height,
        transport,
        land_mask,
        sea_depth,
        baro,
        still_s,
        still_n,
        still_w,
        still_e,
        *halo,
    )
    return (height, flow, new_tracers.reshape(tracers.shape))


def solution(mesh):
    in_specs = (
        P(None, AXES),
        P(AXES, None),
        P(AXES, None),
        P(AXES, None),
        P(AXES, None),
        P(("comp", "ty"), "tx"),
        P(("comp", "ty"), "tx"),
        P(("comp", "ty"), "tx"),
        P(None, ("comp", "ty"), "tx"),
        P(None, None, ("comp", "ty"), "tx"),
    )
    out_specs = (
        P(("comp", "ty"), "tx"),
        P(None, ("comp", "ty"), "tx"),
        P(None, None, ("comp", "ty"), "tx"),
    )
    ny = mesh.shape["comp"] * mesh.shape["ty"]
    nx = mesh.shape["tx"]
    body = functools.partial(local, ny, nx)
    return jax.shard_map(body, mesh=mesh, in_specs=in_specs, out_specs=out_specs, check_vma=False)
```

profile of v0, /device:TPU:19, one launch (start us, length us, event | category | flops | bytes accessed | tf_op | source)
XLA Modules:
  0.0 175.6 jit_solution(11663197161247760547)
XLA Ops:
  0.6 5.7 %pack.1 = f32[32,144,128]{2,1,0:T(8,128)} custom-call(s32[256]{0:T(256)} %bitcast.37, f32[8,16384]{1,0:T(8,128)} %flux_ref.1, s32[256,128]{1,0:T(8,128)} %src_ref.1, s32[256,128]{1,0:T(8,128)} %cell_ref.1, f32[256,128]{1,0:T(8,128)} %weight_ref.1), custom_call_target="tpu_custom_call" | custom-call | flops 10000000 | bytes 4000000 | tf_op jit(solution)/shard_map/pack/pallas_call | solution.py:71
  6.3 6.2 %all-to-all-start = ((f32[32,144,128]{2,1,0:T(8,128)}), f32[32,144,128]{2,1,0:T(8,128)S(1)}, u32[]{:S(2)}, u32[]{:S(2)}) async-start(f32[32,144,128]{2,1,0:T(8,128)} %pack.1), calls=%async_computation | async-start | bytes 4718592 | tf_op jit(solution)/shard_map/all_to_all | solution.py:496
  12.6 0.0 copy-start.1
  12.6 0.0 copy-start
  12.6 0.0 copy-start.2
  12.6 0.0 copy-start.4
  12.6 8.3 %copy.17 = f32[2,16,64,1024]{3,1,0,2:T(8,128)S(1)} copy(f32[2,16,64,1024]{3,2,1,0:T(8,128)} %param.19) | data formatting | bytes 16777216 | tf_op args[9]
  21.1 2.2 %collective-permute-start.1 = (f32[72,1024]{1,0:T(8,128)S(1)}, f32[72,1024]{1,0:T(8,128)S(1)}, u32[]{:S(2)}, u32[]{:S(2)}) collective-permute-start(f32[72,1024]{1,0:T(8,128)S(1)} %pad_maximum_fusion.1), channel_id=1, source_target_pairs={{4,0},{5,1},{6,2},{7,3},{8,4},{9,5},{10,6},{11,7},{12,8},{13,9},{1... | collective-permute-start | bytes 884744 | tf_op jit(solution)/shard_map/ppermute | solution.py:465
  23.3 3.1 %collective-permute-start = (f32[72,1024]{1,0:T(8,128)S(1)}, f32[72,1024]{1,0:T(8,128)S(1)}, u32[]{:S(2)}, u32[]{:S(2)}) collective-permute-start(f32[72,1024]{1,0:T(8,128)S(1)} %pad_maximum_fusion), channel_id=1, source_target_pairs={{0,4},{1,5},{2,6},{3,7},{4,8},{5,9},{6,10},{7,11},{8,12},{9,13},{1... | collective-permute-start | bytes 884744 | tf_op jit(solution)/shard_map/ppermute | solution.py:465
  26.4 2.8 %edges.1 = (f32[64,128]{1,0:T(8,128)}, f32[64,128]{1,0:T(8,128)}) custom-call(f32[32,64,1024]{2,1,0:T(8,128)} %bitcast.24, f32[32,64,1024]{2,1,0:T(8,128)} %bitcast.25, s32[64,1024]{1,0:T(8,128)} %mask_ref.3, s32[64,1024]{1,0:T(8,128)} %mask_ref.3), custom_call_target="tpu_custom_call" | custom-call | tf_op jit(solution)/shard_map/edges/pallas_call | solution.py:186
  29.3 46.8 %collective-permute-done.1 = f32[72,1024]{1,0:T(8,128)S(1)} collective-permute-done((f32[72,1024]{1,0:T(8,128)S(1)}, f32[72,1024]{1,0:T(8,128)S(1)}, u32[]{:S(2)}, u32[]{:S(2)}) %collective-permute-start.1) | collective-permute-done | bytes 294944 | tf_op jit(solution)/shard_map/ppermute | solution.py:465
  76.0 0.0 collective-permute-done
  76.0 0.7 copy-done.7
  76.8 1.6 pad_maximum_fusion.2
  78.4 1.3 collective-permute-start.2
  79.6 1.5 pad_maximum_fusion.3
  81.1 4.1 %collective-permute-start.3 = (f32[464,128]{1,0:T(8,128)}, f32[464,128]{1,0:T(8,128)}, u32[]{:S(2)}, u32[]{:S(2)}) collective-permute-start(f32[464,128]{1,0:T(8,128)} %pad_maximum_fusion.3), channel_id=1, source_target_pairs={{1,0},{2,1},{3,2},{5,4},{6,5},{7,6},{9,8},{10,9},{11,10},{13,12},{... | collective-permute-start | bytes 712712 | tf_op jit(solution)/shard_map/ppermute | solution.py:465
  85.2 0.0 all-to-all-done.in_ref
  85.2 0.6 fusion
  85.9 0.1 convert_element_type.11
  85.9 0.7 add_select_fusion.row_ref
  86.6 0.1 copy-done.3
  86.6 21.0 %scatter.1 = (f32[8,64,1024]{2,1,0:T(8,128)}, f32[4,64,1024]{2,1,0:T(8,128)}) custom-call(s32[512]{0:T(512)} %add_select_fusion.row_ref, f32[32,144,128]{2,1,0:T(8,128)} %copy-done.3), custom_call_target="tpu_custom_call" | custom-call | flops 2000000000 | bytes 5000000 | tf_op jit(solution)/shard_map/scatter/pallas_call | solution.py:148
  107.6 1.0 fusion.6
  108.6 1.0 fusion.5
  109.6 1.9 %collective-permute-start.4 = (f32[4,8,1024]{2,1,0:T(8,128)S(1)}, f32[4,8,1024]{2,1,0:T(8,128)S(1)}, u32[]{:S(2)}, u32[]{:S(2)}) collective-permute-start(f32[4,8,1024]{2,1,0:T(8,128)S(1)} %get-tuple-element.28), channel_id=1, source_target_pairs={{0,4},{1,5},{2,6},{3,7},{4,8},{5,9},{6,10},{7,11},{8,12},{9,13},{1... | collective-permute-start | bytes 393224 | tf_op jit(solution)/shard_map/ppermute | solution.py:465
  111.5 4.3 %collective-permute-start.5 = (f32[4,8,1024]{2,1,0:T(8,128)S(1)}, f32[4,8,1024]{2,1,0:T(8,128)S(1)}, u32[]{:S(2)}, u32[]{:S(2)}) collective-permute-start(f32[4,8,1024]{2,1,0:T(8,128)S(1)} %get-tuple-element.27), channel_id=1, source_target_pairs={{4,0},{5,1},{6,2},{7,3},{8,4},{9,5},{10,6},{11,7},{12,8},{13,9},{1... | collective-permute-start | bytes 393224 | tf_op jit(solution)/shard_map/ppermute | solution.py:465
  115.8 1.3 collective-permute-start.6
  117.1 0.0 collective-permute-done.2
  117.1 3.7 %collective-permute-start.7 = (f32[4,64,128]{2,1,0:T(8,128)S(1)}, f32[4,64,128]{2,1,0:T(8,128)S(1)}, u32[]{:S(2)}, u32[]{:S(2)}) collective-permute-start(f32[4,64,128]{2,1,0:T(8,128)S(1)} %get-tuple-element.25), channel_id=1, source_target_pairs={{1,0},{2,1},{3,2},{5,4},{6,5},{7,6},{9,8},{10,9},{11,10},{13,12},{... | collective-permute-start | bytes 393224 | tf_op jit(solution)/shard_map/ppermute | solution.py:465
  120.8 0.8 fusion.4
  121.6 0.0 collective-permute-done.3
  121.6 1.3 collective-permute-start.10
  122.9 3.8 %collective-permute-done.10.fnw_ref = f32[4,8,128]{2,1,0:T(8,128)S(1)} collective-permute-done((f32[4,8,128]{2,1,0:T(8,128)S(1)}, f32[4,8,128]{2,1,0:T(8,128)S(1)}, u32[]{:S(2)}, u32[]{:S(2)}) %collective-permute-start.10) | collective-permute-done | bytes 16416 | tf_op jit(solution)/shard_map/ppermute | solution.py:465
  126.7 6.1 %collective-permute-start.11 = (f32[4,8,128]{2,1,0:T(8,128)S(1)}, f32[4,8,128]{2,1,0:T(8,128)S(1)}, u32[]{:S(2)}, u32[]{:S(2)}) collective-permute-start(f32[4,8,128]{2,1,0:T(8,128)S(1)} %get-tuple-element.21), channel_id=1, source_target_pairs={{5,0},{6,1},{7,2},{9,4},{10,5},{11,6},{13,8},{14,9},{15,10},{17,12... | collective-permute-start | bytes 49160 | tf_op jit(solution)/shard_map/ppermute | solution.py:465
  132.8 0.9 collective-permute-done.11.fne_ref
  133.7 1.3 collective-permute-start.8
  135.0 4.6 %collective-permute-done.8.fsw_ref = f32[4,8,128]{2,1,0:T(8,128)S(1)} collective-permute-done((f32[4,8,128]{2,1,0:T(8,128)S(1)}, f32[4,8,128]{2,1,0:T(8,128)S(1)}, u32[]{:S(2)}, u32[]{:S(2)}) %collective-permute-start.8) | collective-permute-done | bytes 16416 | tf_op jit(solution)/shard_map/ppermute | solution.py:465
  139.6 7.5 %collective-permute-start.9 = (f32[4,8,128]{2,1,0:T(8,128)S(1)}, f32[4,8,128]{2,1,0:T(8,128)S(1)}, u32[]{:S(2)}, u32[]{:S(2)}) collective-permute-start(f32[4,8,128]{2,1,0:T(8,128)S(1)} %get-tuple-element.23), channel_id=1, source_target_pairs={{1,4},{2,5},{3,6},{5,8},{6,9},{7,10},{9,12},{10,13},{11,14},{13,16... | collective-permute-start | bytes 49160 | tf_op jit(solution)/shard_map/ppermute | solution.py:465
  147.1 0.0 copy-done.10
  147.1 0.7 slice.114.south_ref
  147.7 0.7 slice.115.north_ref
  148.4 0.6 slice.118.mask_south_ref
  149.0 0.6 slice.119.mask_north_ref
  149.6 1.6 slice.112
  151.2 1.4 slice.116.west_ref
  152.6 1.6 slice.113
  154.2 1.4 slice.117.east_ref
  155.6 14.3 %tracer.1 = f32[32,64,1024]{2,1,0:T(8,128)} custom-call(f32[32,64,1024]{2,1,0:T(8,128)} %bitcast.26, f32[32,1024]{1,0:T(8,128)} %slice.114.south_ref, f32[32,1024]{1,0:T(8,128)} %slice.115.north_ref, f32[64,128]{1,0:T(8,128)} %slice.116.west_ref, f32[64,128]{1,0:T(8,128)} %slice.117.east_ref, f32[8,1024]{1,0:T(8,128)} %slice.118.mask_south_ref, ...), custom_call_target="tpu_custom_call" | custom-call | flops 100000000 | bytes 40000000 | tf_op jit(solution)/shard_map/tracer/pallas_call | solution.py:346
  169.9 0.0 copy-done.5
  169.9 0.0 copy-done.15
  169.9 0.0 copy-done.16
  169.9 0.0 copy-done.17
  170.0 0.0 collective-permute-done.9.fse_ref
  170.0 0.0 collective-permute-done.4.fs_ref
  170.0 0.0 collective-permute-done.5.fn_ref
  170.0 0.0 collective-permute-done.6.fw_ref
  170.0 0.0 collective-permute-done.7.fe_ref
  170.1 0.5 copy-done.18
  170.6 0.1 copy-done.11
  170.6 0.1 copy-done.12
  170.7 0.0 copy-done.13
  170.7 0.1 copy-done.14
  170.8 4.8 %baro.1 = (f32[64,1024]{1,0:T(8,128)}, f32[2,64,1024]{2,1,0:T(8,128)}) custom-call(f32[64,1024]{1,0:T(8,128)} %height_ref.1, f32[2,64,1024]{2,1,0:T(8,128)} %flow_ref.3, s32[64,1024]{1,0:T(8,128)} %mask_ref.3, f32[64,1024]{1,0:T(8,128)} %depth_ref.3, f32[4,64,1024]{2,1,0:T(8,128)} %get-tuple-element.9.baro_ref, f32[5,8,1024]{2,1,0:T(8,128)} %copy-done.6, ...), custom_call_target="tpu_custom_call" | custom-call | tf_op jit(solution)/shard_map/baro/pallas_call | solution.py:528
  (30 shorter events, 0.2 us)
Async XLA Ops:
  6.3 78.9 %all-to-all-start = ((f32[32,144,128]{2,1,0:T(8,128)}), f32[32,144,128]{2,1,0:T(8,128)S(1)}, u32[]{:S(2)}, u32[]{:S(2)}) async-start(f32[32,144,128]{2,1,0:T(8,128)} %pack.1), calls=%async_computation | async-start | bytes 4718592 | tf_op jit(solution)/shard_map/all_to_all | solution.py:496
  12.6 8.4 %copy-start.1 = (s32[64,1024]{1,0:T(8,128)S(1)}, s32[64,1024]{1,0:T(8,128)}, u32[]{:S(2)}) copy-start(s32[64,1024]{1,0:T(8,128)} %mask_ref.3) | copy-start | bytes 786436
  12.6 8.4 %copy-start = (f32[2,64,1024]{2,1,0:T(8,128)S(1)}, f32[2,64,1024]{2,1,0:T(8,128)}, u32[]{:S(2)}) copy-start(f32[2,64,1024]{2,1,0:T(8,128)} %flow_ref.3) | copy-start | bytes 1572868
  12.6 8.4 %copy-start.2 = (f32[64,1024]{1,0:T(8,128)S(1)}, f32[64,1024]{1,0:T(8,128)}, u32[]{:S(2)}) copy-start(f32[64,1024]{1,0:T(8,128)} %depth_ref.3) | copy-start | bytes 786436
  12.6 8.4 %copy-start.4 = (f32[64,1024]{1,0:T(8,128)S(1)}, f32[64,1024]{1,0:T(8,128)}, u32[]{:S(2)}) copy-start(f32[64,1024]{1,0:T(8,128)} %height_ref.1) | copy-start | bytes 786436
  21.1 54.9 %collective-permute-start.1 = (f32[72,1024]{1,0:T(8,128)S(1)}, f32[72,1024]{1,0:T(8,128)S(1)}, u32[]{:S(2)}, u32[]{:S(2)}) collective-permute-start(f32[72,1024]{1,0:T(8,128)S(1)} %pad_maximum_fusion.1), channel_id=1, source_target_pairs={{4,0},{5,1},{6,2},{7,3},{8,4},{9,5},{10,6},{11,7},{12,8},{13,9},{1... | collective-permute-start | bytes 884744 | tf_op jit(solution)/shard_map/ppermute | solution.py:465
  23.3 52.7 %collective-permute-start = (f32[72,1024]{1,0:T(8,128)S(1)}, f32[72,1024]{1,0:T(8,128)S(1)}, u32[]{:S(2)}, u32[]{:S(2)}) collective-permute-start(f32[72,1024]{1,0:T(8,128)S(1)} %pad_maximum_fusion), channel_id=1, source_target_pairs={{0,4},{1,5},{2,6},{3,7},{4,8},{5,9},{6,10},{7,11},{8,12},{9,13},{1... | collective-permute-start | bytes 884744 | tf_op jit(solution)/shard_map/ppermute | solution.py:465
  76.0 0.7 copy-start.7
  76.0 93.9 %copy-start.5 = (f32[5,8,1024]{2,1,0:T(8,128)}, f32[5,8,1024]{2,1,0:T(8,128)S(1)}, u32[]{:S(2)}) copy-start(f32[5,8,1024]{2,1,0:T(8,128)S(1)} %slice_bitcast_fusion.north_ref) | copy-start | bytes 491524
  76.7 4.4 %copy-start.9 = (f32[72,1024]{1,0:T(8,128)}, f32[72,1024]{1,0:T(8,128)S(1)}, u32[]{:S(2)}) copy-start(f32[72,1024]{1,0:T(8,128)S(1)} %collective-permute-done) | copy-start | bytes 884740
  76.7 4.4 %copy-start.6 = (f32[5,8,1024]{2,1,0:T(8,128)}, f32[5,8,1024]{2,1,0:T(8,128)S(1)}, u32[]{:S(2)}) copy-start(f32[5,8,1024]{2,1,0:T(8,128)S(1)} %slice_bitcast_fusion.1.south_ref) | copy-start | bytes 491524
  76.8 71.0 %copy-start.8 = (f32[72,1024]{1,0:T(8,128)S(1)}, f32[72,1024]{1,0:T(8,128)}, u32[]{:S(2)}) copy-start(f32[72,1024]{1,0:T(8,128)} %copy-done.7) | copy-start | bytes 884740
  78.4 38.7 %collective-permute-start.2 = (f32[464,128]{1,0:T(8,128)}, f32[464,128]{1,0:T(8,128)}, u32[]{:S(2)}, u32[]{:S(2)}) collective-permute-start(f32[464,128]{1,0:T(8,128)} %pad_maximum_fusion.2), channel_id=1, source_target_pairs={{0,1},{1,2},{2,3},{4,5},{5,6},{6,7},{8,9},{9,10},{10,11},{12,13},{... | collective-permute-start | bytes 712712 | tf_op jit(solution)/shard_map/ppermute | solution.py:465
  81.1 40.5 %collective-permute-start.3 = (f32[464,128]{1,0:T(8,128)}, f32[464,128]{1,0:T(8,128)}, u32[]{:S(2)}, u32[]{:S(2)}) collective-permute-start(f32[464,128]{1,0:T(8,128)} %pad_maximum_fusion.3), channel_id=1, source_target_pairs={{1,0},{2,1},{3,2},{5,4},{6,5},{7,6},{9,8},{10,9},{11,10},{13,12},{... | collective-permute-start | bytes 712712 | tf_op jit(solution)/shard_map/ppermute | solution.py:465
  85.2 61.8 %copy-start.10 = (f32[72,1024]{1,0:T(8,128)S(1)}, f32[72,1024]{1,0:T(8,128)}, u32[]{:S(2)}) copy-start(f32[72,1024]{1,0:T(8,128)} %copy-done.9) | copy-start | bytes 884740
  85.2 1.4 copy-start.3
  109.6 60.4 %collective-permute-start.4 = (f32[4,8,1024]{2,1,0:T(8,128)S(1)}, f32[4,8,1024]{2,1,0:T(8,128)S(1)}, u32[]{:S(2)}, u32[]{:S(2)}) collective-permute-start(f32[4,8,1024]{2,1,0:T(8,128)S(1)} %get-tuple-element.28), channel_id=1, source_target_pairs={{0,4},{1,5},{2,6},{3,7},{4,8},{5,9},{6,10},{7,11},{8,12},{9,13},{1... | collective-permute-start | bytes 393224 | tf_op jit(solution)/shard_map/ppermute | solution.py:465
  111.5 58.5 %collective-permute-start.5 = (f32[4,8,1024]{2,1,0:T(8,128)S(1)}, f32[4,8,1024]{2,1,0:T(8,128)S(1)}, u32[]{:S(2)}, u32[]{:S(2)}) collective-permute-start(f32[4,8,1024]{2,1,0:T(8,128)S(1)} %get-tuple-element.27), channel_id=1, source_target_pairs={{4,0},{5,1},{6,2},{7,3},{8,4},{9,5},{10,6},{11,7},{12,8},{13,9},{1... | collective-permute-start | bytes 393224 | tf_op jit(solution)/shard_map/ppermute | solution.py:465
  115.8 54.2 %collective-permute-start.6 = (f32[4,64,128]{2,1,0:T(8,128)S(1)}, f32[4,64,128]{2,1,0:T(8,128)S(1)}, u32[]{:S(2)}, u32[]{:S(2)}) collective-permute-start(f32[4,64,128]{2,1,0:T(8,128)S(1)} %get-tuple-element.26), channel_id=1, source_target_pairs={{0,1},{1,2},{2,3},{4,5},{5,6},{6,7},{8,9},{9,10},{10,11},{12,13},{... | collective-permute-start | bytes 393224 | tf_op jit(solution)/shard_map/ppermute | solution.py:465
  117.1 52.9 %collective-permute-start.7 = (f32[4,64,128]{2,1,0:T(8,128)S(1)}, f32[4,64,128]{2,1,0:T(8,128)S(1)}, u32[]{:S(2)}, u32[]{:S(2)}) collective-permute-start(f32[4,64,128]{2,1,0:T(8,128)S(1)} %get-tuple-element.25), channel_id=1, source_target_pairs={{1,0},{2,1},{3,2},{5,4},{6,5},{7,6},{9,8},{10,9},{11,10},{13,12},{... | collective-permute-start | bytes 393224 | tf_op jit(solution)/shard_map/ppermute | solution.py:465
  121.6 5.1 %collective-permute-start.10 = (f32[4,8,128]{2,1,0:T(8,128)S(1)}, f32[4,8,128]{2,1,0:T(8,128)S(1)}, u32[]{:S(2)}, u32[]{:S(2)}) collective-permute-start(f32[4,8,128]{2,1,0:T(8,128)S(1)} %get-tuple-element.22), channel_id=1, source_target_pairs={{4,1},{5,2},{6,3},{8,5},{9,6},{10,7},{12,9},{13,10},{14,11},{16,13... | collective-permute-start | bytes 49160 | tf_op jit(solution)/shard_map/ppermute | solution.py:465
  126.7 43.3 %copy-start.15 = (f32[4,8,128]{2,1,0:T(8,128)}, f32[4,8,128]{2,1,0:T(8,128)S(1)}, u32[]{:S(2)}) copy-start(f32[4,8,128]{2,1,0:T(8,128)S(1)} %collective-permute-done.10.fnw_ref) | copy-start | bytes 49156
  126.7 7.0 %collective-permute-start.11 = (f32[4,8,128]{2,1,0:T(8,128)S(1)}, f32[4,8,128]{2,1,0:T(8,128)S(1)}, u32[]{:S(2)}, u32[]{:S(2)}) collective-permute-start(f32[4,8,128]{2,1,0:T(8,128)S(1)} %get-tuple-element.21), channel_id=1, source_target_pairs={{5,0},{6,1},{7,2},{9,4},{10,5},{11,6},{13,8},{14,9},{15,10},{17,12... | collective-permute-start | bytes 49160 | tf_op jit(solution)/shard_map/ppermute | solution.py:465
  133.7 36.3 %copy-start.16 = (f32[4,8,128]{2,1,0:T(8,128)}, f32[4,8,128]{2,1,0:T(8,128)S(1)}, u32[]{:S(2)}) copy-start(f32[4,8,128]{2,1,0:T(8,128)S(1)} %collective-permute-done.11.fne_ref) | copy-start | bytes 49156
  133.7 5.9 %collective-permute-start.8 = (f32[4,8,128]{2,1,0:T(8,128)S(1)}, f32[4,8,128]{2,1,0:T(8,128)S(1)}, u32[]{:S(2)}, u32[]{:S(2)}) collective-permute-start(f32[4,8,128]{2,1,0:T(8,128)S(1)} %get-tuple-element.24), channel_id=1, source_target_pairs={{0,5},{1,6},{2,7},{4,9},{5,10},{6,11},{8,13},{9,14},{10,15},{12,17... | collective-permute-start | bytes 49160 | tf_op jit(solution)/shard_map/ppermute | solution.py:465
  139.6 30.4 %copy-start.17 = (f32[4,8,128]{2,1,0:T(8,128)}, f32[4,8,128]{2,1,0:T(8,128)S(1)}, u32[]{:S(2)}) copy-start(f32[4,8,128]{2,1,0:T(8,128)S(1)} %collective-permute-done.8.fsw_ref) | copy-start | bytes 49156
  139.6 30.4 %collective-permute-start.9 = (f32[4,8,128]{2,1,0:T(8,128)S(1)}, f32[4,8,128]{2,1,0:T(8,128)S(1)}, u32[]{:S(2)}, u32[]{:S(2)}) collective-permute-start(f32[4,8,128]{2,1,0:T(8,128)S(1)} %get-tuple-element.23), channel_id=1, source_target_pairs={{1,4},{2,5},{3,6},{5,8},{6,9},{7,10},{9,12},{10,13},{11,14},{13,16... | collective-permute-start | bytes 49160 | tf_op jit(solution)/shard_map/ppermute | solution.py:465
  170.0 0.6 copy-start.18
  170.0 0.6 copy-start.11
  170.0 0.7 copy-start.12
  170.0 0.7 copy-start.13
  170.1 0.7 copy-start.14
where the time goes:
time: 177 us; the launch traced here: 176 us
  waiting for transfers between devices  56 us (32%)
  Pallas kernels  48.6 us (27%)
  starting transfers between devices  44.3 us (25%)
  local copies, waits for them, and re-layouts  21.2 us (12%)
  other arithmetic  4.42 us (2%)
    ppermute x12, waiting for transfers between devices, from_side(): return lax.ppermute(a, AXES, perm)  56 us
    ppermute x12, starting transfers between devices, from_side(): return lax.ppermute(a, AXES, perm)  38.1 us
    pallas_call x1, Pallas kernels, scatter(): pl.pallas_call(functools.partial(scatter_kernel, cap, fields), out_shape=...  21 us
    pallas_call x1, Pallas kernels, tracer_step(): pl.pallas_call(functools.partial(tracer_kernel, levels), out_shape=jax.Sh...  14.3 us
    unnamed x39, local copies, waits for them, and re-layouts  9.86 us
    all_to_all x1, starting transfers between devices, local(): lax.all_to_all(outgoing, AXES, split_axis=0, concat_axis=0, tiled=True)  6.22 us
    pallas_call x1, Pallas kernels, pack(): pl.pallas_call(functools.partial(pack_kernel, cap), out_shape=jax.ShapeDt...  5.7 us
    pallas_call x1, Pallas kernels, local(): pl.pallas_call(baro_kernel, out_shape=(jax.ShapeDtypeStruct(sea_height.sh...  4.77 us
  transfers between devices with their start and end apart: 13, of which 4 were waited for; matrix products, arithmetic and copies ran while one was open for 14% of the time, Pallas kernels for 22%

commit v1 on v0

--- a/solution.py
+++ b/solution.py
@@ -29,14 +29,17 @@
     return pl.BlockSpec(memory_space=pltpu.SMEM)
 
 
-def pack_kernel(cap, tile_ref, flux_ref, src_ref, cell_ref, weight_ref, out_ref, count_ref):
-    tiles = out_ref.shape[0]
+def pack_kernel(cap, tile_ref, flux_ref, src_ref, cell_ref, weight_ref, *rest):
+    *parts, out_ref, count_ref = rest
+    tiles = parts[0].shape[0]
+    share = cap // len(parts)
     blocks = src_ref.shape[0]
     fields = flux_ref.shape[0]
     width = src_ref.shape[1]
 
     def clear(t, carry):
-        out_ref[t] = jnp.zeros(out_ref.shape[1:], f32)
+        for c in range(len(parts)):
+            out_ref[c * tiles + t] = jnp.zeros(out_ref.shape[1:], f32)
         count_ref[t] = 0
         return carry
 
@@ -57,39 +60,57 @@
                 t = tile_ref[base + j]
                 r = count_ref[t]
                 count_ref[t] = r + 1
-                at = pl.multiple_of(r * fields, fields)
-                out_ref[t, pl.ds(at, fields), :] = picked * weights[j : j + 1]
-                out_ref[t, pl.ds(cap * fields + r, 1), :] = cells[j : j + 1]
+                slot = r % share
+                lead = (r // share) * tiles + t
+                at = pl.multiple_of(slot * fields, fields)
+                out_ref[lead, pl.ds(at, fields), :] = picked * weights[j : j + 1]
+                out_ref[lead, pl.ds(share * fields + slot, 1), :] = cells[j : j + 1]
         return carry
 
     lax.fori_loop(0, blocks // 8, group, 0)
-
-
-def pack(margin_tile, atm_flux, margin_source, margin_cell, margin_weight, tiles, cap):
+    for c, part in enumerate(parts):
+
+        def move(t, carry, c=c, part=part):
+            part[t] = out_ref[c * tiles + t]
+            return carry
+
+        lax.fori_loop(0, tiles, move, 0)
+
+
+def pack(margin_tile, atm_flux, margin_source, margin_cell, margin_weight, tiles, cap, parts):
     fields = atm_flux.shape[0]
-    rows = cap * fields + -(-cap // 8) * 8
+    share = cap // parts
+    rows = share * fields + -(-share // 8) * 8
+    width = margin_source.shape[1]
     return pl.pallas_call(
         functools.partial(pack_kernel, cap),
-        out_shape=jax.ShapeDtypeStruct((tiles, rows, margin_source.shape[1]), f32),
+        out_shape=[jax.ShapeDtypeStruct((tiles, rows, width), f32)] * parts,
         in_specs=[smem(), vmem(), vmem(), vmem(), vmem()],
-        out_specs=vmem(),
-        scratch_shapes=[pltpu.SMEM((tiles,), jnp.int32)],
+        out_specs=[vmem()] * parts,
+        scratch_shapes=[
+            pltpu.VMEM((parts * tiles, rows, width), f32),
+            pltpu.SMEM((tiles,), jnp.int32),
+        ],
         compiler_params=pltpu.CompilerParams(vmem_limit_bytes=VMEM_LIMIT),
         cost_estimate=pl.CostEstimate(flops=10_000_000, bytes_accessed=4_000_000, transcendentals=0),
         name="pack",
     )(margin_tile, atm_flux, margin_source, margin_cell, margin_weight)
 
 
-def scatter_kernel(cap, fields, row_ref, in_ref, forcing_ref, baro_ref, acc_ref):
+def scatter_kernel(cap, fields, tile_rows, tile_cols, start, finish, row_ref, in_ref, *rest):
+    if finish:
+        forcing_ref, baro_ref, acc_ref = rest[-3:]
+    else:
+        acc_ref = rest[-1]
     owners = in_ref.shape[0]
     width = in_ref.shape[2]
-    tile_rows, tile_cols = forcing_ref.shape[1:]
     highs = tile_cols // LANES
     lines = highs * fields
     group = 4 if cap % 4 == 0 else 1
 
     def clear(y, carry):
-        acc_ref[pl.ds(pl.multiple_of(y * lines, lines), lines), :] = jnp.zeros((lines, LANES), f32)
+        at = pl.ds(pl.multiple_of(y * lines, lines), lines)
+        acc_ref[at, :] = jnp.zeros((lines, LANES), f32) if start else rest[0][at, :]
         return carry
 
     lax.fori_loop(0, tile_rows, clear, 0)
@@ -125,6 +146,9 @@
 
     lax.fori_loop(0, owners, owner_step, 0)
 
+    if not finish:
+        return
+
     def unfold(yb, carry):
         ys = pl.ds(pl.multiple_of(yb * 8, 8), 8)
         for h in range(highs):
@@ -143,26 +167,37 @@
     lax.fori_loop(0, tile_rows // 8, unfold, 0)
 
 
-def scatter(rows, arrived, cap, fields, tile_rows, tile_cols):
+def scatter(rows, arrived, total, cap, fields, tile_rows, tile_cols, finish):
     lines = tile_cols // LANES * fields
-    return pl.pallas_call(
-        functools.partial(scatter_kernel, cap, fields),
-        out_shape=(
+    sums = (tile_rows * lines, LANES)
+    extra = [] if total is None else [total]
+    if finish:
+        out_shape = [
             jax.ShapeDtypeStruct((fields, tile_rows, tile_cols), f32),
             jax.ShapeDtypeStruct((4, tile_rows, tile_cols), f32),
-        ),
-        in_specs=[smem(), vmem()],
-        out_specs=(vmem(), vmem()),
-        scratch_shapes=[pltpu.VMEM((tile_rows * lines, LANES), f32)],
+        ]
+    else:
+        out_shape = [jax.ShapeDtypeStruct(sums, f32)]
+    return pl.pallas_call(
+        functools.partial(
+            scatter_kernel, cap, fields, tile_rows, tile_cols, total is None, finish
+        ),
+        out_shape=out_shape,
+        in_specs=[smem(), vmem()] + [vmem()] * len(extra),
+        out_specs=[vmem()] * len(out_shape),
+        scratch_shapes=[pltpu.VMEM(sums, f32)] if finish else [],
         compiler_params=pltpu.CompilerParams(vmem_limit_bytes=VMEM_LIMIT),
         cost_estimate=pl.CostEstimate(
-            flops=2_000_000_000, bytes_accessed=5_000_000, transcendentals=0
+            flops=2_000_000_000, bytes_accessed=20_000_000, transcendentals=0
         ),
         name="scatter",
-    )(rows, arrived)
-
-
-def edges_kernel(west_ref, east_ref, mask_west_ref, mask_east_ref, first_ref, last_ref):
+    )(rows, arrived, *extra)
+
+
+def edges_kernel(
+    west_ref, east_ref, low_ref, high_ref, mask_west_ref, mask_east_ref,
+    first_ref, last_ref, bottom_ref, top_ref,
+):
     planes, rows = west_ref.shape[:2]
     lane = lax.broadcasted_iota(jnp.int32, (rows, LANES), 1)
     for src, mask, dst, col in (
@@ -176,31 +211,139 @@
             )
         edge = mask[:, col : col + 1].astype(f32)
         dst[...] = jnp.where(lane == planes, jnp.broadcast_to(edge, (rows, LANES)), total)
-
-
-def edge_columns(tracers, land_mask):
+    for p in range(planes):
+        bottom_ref[p : p + 1, :] = low_ref[p, 0:1, :]
+        top_ref[p : p + 1, :] = high_ref[p, 7:8, :]
+
+
+def tracer_edges(tracers, land_mask):
     planes, rows, cols = tracers.shape
     end = cols // LANES - 1
+    top = rows // 8 - 1
     strip = jax.ShapeDtypeStruct((rows, LANES), f32)
+    line = jax.ShapeDtypeStruct((planes, cols), f32)
     whole = pl.BlockSpec((rows, LANES), lambda i: (0, 0))
+    wide = pl.BlockSpec((planes, cols), lambda i: (0, 0))
     return pl.pallas_call(
         edges_kernel,
-        out_shape=(strip, strip),
+        out_shape=(strip, strip, line, line),
         grid=(1,),
         in_specs=[
             pl.BlockSpec((planes, rows, LANES), lambda i: (0, 0, 0)),
             pl.BlockSpec((planes, rows, LANES), lambda i: (0, 0, end)),
+            pl.BlockSpec((planes, 8, cols), lambda i: (0, 0, 0)),
+            pl.BlockSpec((planes, 8, cols), lambda i: (0, top, 0)),
             pl.BlockSpec((rows, LANES), lambda i: (0, 0)),
             pl.BlockSpec((rows, LANES), lambda i: (0, end)),
         ],
-        out_specs=(whole, whole),
+        out_specs=(whole, whole, wide, wide),
         compiler_params=pltpu.CompilerParams(vmem_limit_bytes=VMEM_LIMIT),
+        cost_estimate=pl.CostEstimate(flops=1_000_000, bytes_accessed=5_000_000, transcendentals=0),
         name="edges",
-    )(tracers, tracers, land_mask, land_mask)
-
-
-def tracer_kernel(
-    levels,
+    )(tracers, tracers, tracers, tracers, land_mask, land_mask)
+
+
+WAYS = ((1, 0), (-1, 0), (0, 1), (0, -1), (1, 1), (1, -1), (-1, 1), (-1, -1))
+
+
+def exchange_kernel(mesh_shape, extras, *refs):
+    comps, depth, nx = mesh_shape
+    ny = comps * depth
+    band, lines = refs[0], refs[1 : 1 + extras]
+    outs = refs[1 + extras : 1 + 2 * extras + len(WAYS)]
+    send_sems, recv_sems = refs[-2:]
+    rows, cols = band.shape[1:]
+    y = lax.axis_index("comp") * depth + lax.axis_index("ty")
+    x = lax.axis_index("tx")
+
+    def inside(dy, dx):
+        return (y + dy >= 0) & (y + dy < ny) & (x + dx >= 0) & (x + dx < nx)
+
+    def place(dy, dx):
+        return ((y + dy) // depth, (y + dy) % depth, x + dx)
+
+    barrier = pltpu.get_barrier_semaphore()
+    near = jnp.int32(0)
+    for way in WAYS:
+        near = near + inside(*way).astype(jnp.int32)
+
+        @pl.when(inside(*way))
+        def _(way=way):
+            pl.semaphore_signal(
+                barrier, inc=1, device_id=place(*way), device_id_type=pl.DeviceIdType.MESH
+            )
+
+    pl.semaphore_wait(barrier, near)
+
+    def pieces():
+        for k, (dy, dx) in enumerate(WAYS):
+            start_y = rows - RIM if dy == 1 else 0
+            start_x = cols - LANES if dx == 1 else 0
+            tall = RIM if dy else rows
+            wide = LANES if dx else cols
+            yield (dy, dx), band.at[:, pl.ds(start_y, tall), pl.ds(start_x, wide)]
+        for k in range(extras):
+            yield WAYS[k], lines[k]
+
+    copies = []
+    for k, (way, src) in enumerate(pieces()):
+        dst = outs[k]
+
+        def copy(way=way, src=src, dst=dst, k=k):
+            return pltpu.make_async_remote_copy(
+                src_ref=src,
+                dst_ref=dst,
+                send_sem=send_sems.at[k],
+                recv_sem=recv_sems.at[k],
+                device_id=place(*way),
+                device_id_type=pl.DeviceIdType.MESH,
+            )
+
+        sends, gets = inside(*way), inside(-way[0], -way[1])
+
+        @pl.when(sends)
+        def _(copy=copy):
+            copy().start()
+
+        @pl.when(jnp.logical_not(gets))
+        def _(dst=dst):
+            dst[...] = jnp.zeros(dst.shape, f32)
+
+        copies.append((copy, sends, gets))
+    for copy, sends, gets in copies:
+
+        @pl.when(sends)
+        def _(copy=copy):
+            copy().wait_send()
+
+        @pl.when(gets)
+        def _(copy=copy):
+            copy().wait_recv()
+
+
+def exchange(mesh_shape, band, lines, number):
+    count, rows, cols = band.shape
+    shapes = [
+        (count, RIM if dy else rows, LANES if dx else cols) for dy, dx in WAYS
+    ] + [a.shape for a in lines]
+    return pl.pallas_call(
+        functools.partial(exchange_kernel, mesh_shape, len(lines)),
+        out_shape=[jax.ShapeDtypeStruct(s, f32) for s in shapes],
+        in_specs=[vmem()] * (1 + len(lines)),
+        out_specs=[vmem()] * len(shapes),
+        scratch_shapes=[
+            pltpu.SemaphoreType.DMA((len(shapes),)),
+            pltpu.SemaphoreType.DMA((len(shapes),)),
+        ],
+        compiler_params=pltpu.CompilerParams(
+            collective_id=number, has_side_effects=True, vmem_limit_bytes=VMEM_LIMIT
+        ),
+        cost_estimate=pl.CostEstimate(flops=1000, bytes_accessed=5_000_000, transcendentals=0),
+        name="exchange",
+    )(band, *lines)
+
+
+def advect_kernel(
     tracer_hbm,
     south_ref,
     north_ref,
@@ -211,11 +354,9 @@
     mask_ref,
     depth_ref,
     flow_ref,
-    forcing_ref,
     out_ref,
     held,
     mask_held,
-    ratio_ref,
     sems,
 ):
     planes = held.shape[0]
@@ -284,16 +425,29 @@
     cs = mask_s * (diffuse + advect * jnp.maximum(v, 0.0))
     c0 = 1.0 - (ce + cw + cn + cs)
 
+    ocean = mask > 0.5
+    for p in range(planes):
+        q = held[p, here, :]
+        qe, qw, qn, qs = sides(
+            q, held[p, pl.ds(base + 7, 1), :], held[p, pl.ds(base + 16, 1), :], p
+        )
+        moved = c0 * q + ce * qe + cw * qw + cn * qn + cs * qs
+        out_ref[p] = jnp.where(ocean, moved, q)
+
+
+def solve_kernel(levels, moved_ref, mask_ref, forcing_ref, out_ref, ratio_ref):
     depths = np.arange(levels, dtype=np.float32)
     absorb = np.exp(-depths / np.float32(3)) - np.exp(-(depths + 1) / np.float32(3))
     fade = np.exp(-depths / np.float32(2))
-    stir = 0.5 * forcing_ref[7] * forcing_ref[7]
-    sun = 0.5 * forcing_ref[4]
+    ocean = mask_ref[...].astype(f32)
+    floor = 0.2 * ocean
+    stir = (0.5 * ocean) * forcing_ref[7] * forcing_ref[7]
+    sun = (0.5 * ocean) * forcing_ref[4]
     ratio = None
     last = [None, None]
     lower = None
     for k in range(levels):
-        upper = 0.2 + stir * float(fade[k]) if k < levels - 1 else None
+        upper = floor + stir * float(fade[k]) if k < levels - 1 else None
         pivot = 1.0
         if upper is not None:
             pivot = pivot + upper
@@ -305,46 +459,64 @@
             ratio_ref[k] = ratio
         for t in range(2):
             p = t * levels + k
-            q = held[p, here, :]
-            qe, qw, qn, qs = sides(
-                q, held[p, pl.ds(base + 7, 1), :], held[p, pl.ds(base + 16, 1), :], p
-            )
-            side = c0 * q + ce * qe + cw * qw + cn * qn + cs * qs
+            side = moved_ref[p]
             if t == 0:
                 side = side + sun * float(absorb[k])
                 if k == 0:
-                    side = side + 0.5 * forcing_ref[3]
+                    side = side + (0.5 * ocean) * forcing_ref[3]
             elif k == 0:
-                side = side + (0.5 * forcing_ref[5] - 0.3 * forcing_ref[6])
+                side = side + ocean * (0.5 * forcing_ref[5] - 0.3 * forcing_ref[6])
             if lower is not None:
                 side = side + lower * last[t]
             last[t] = side * scale
             out_ref[p] = last[t]
         lower = upper
-    ocean = mask > 0.5
-    for k in range(levels - 1, -1, -1):
+    for k in range(levels - 2, -1, -1):
         for t in range(2):
             p = t * levels + k
-            if k < levels - 1:
-                last[t] = out_ref[p] - ratio_ref[k] * last[t]
-            out_ref[p] = jnp.where(ocean, last[t], held[p, here, :])
-
-
-def tracer_step(
-    levels, tracers, south, north, west, east, mask_south, mask_north, mask, depth, flow, forcing
-):
-    planes, rows, cols = tracers.shape
+            last[t] = out_ref[p] - ratio_ref[k] * last[t]
+            out_ref[p] = last[t]
+
+
+def solve_step(levels, moved, mask, forcing):
+    planes, rows, cols = moved.shape
 
     def band(*lead):
         zeros = (0,) * len(lead)
         return pl.BlockSpec((*lead, 8, cols), lambda i: (*zeros, i, 0))
 
+    return pl.pallas_call(
+        functools.partial(solve_kernel, levels),
+        out_shape=jax.ShapeDtypeStruct(moved.shape, f32),
+        grid=(rows // 8,),
+        in_specs=[band(planes), band(), band(forcing.shape[0])],
+        out_specs=band(planes),
+        scratch_shapes=[pltpu.VMEM((levels, 8, cols), f32)],
+        compiler_params=pltpu.CompilerParams(
+            vmem_limit_bytes=VMEM_LIMIT, dimension_semantics=("arbitrary",)
+        ),
+        cost_estimate=pl.CostEstimate(
+            flops=30_000_000, bytes_accessed=25_000_000, transcendentals=0
+        ),
+        name="solve",
+    )(moved, mask, forcing)
+
+
+def advect_step(
+    tracers, south, north, west, east, mask_south, mask_north, mask, depth, flow
+):
+    planes, rows, cols = tracers.shape
+
+    def band(*lead):
+        zeros = (0,) * len(lead)
+        return pl.BlockSpec((*lead, 8, cols), lambda i: (*zeros, i, 0))
+
     def full(a):
         zeros = (0,) * a.ndim
         return pl.BlockSpec(a.shape, lambda i: zeros)
 
     return pl.pallas_call(
-        functools.partial(tracer_kernel, levels),
+        advect_kernel,
         out_shape=jax.ShapeDtypeStruct(tracers.shape, f32),
         grid=(rows // 8,),
         in_specs=[
@@ -358,13 +530,11 @@
             full(mask),
             band(),
             band(2),
-            band(forcing.shape[0]),
         ],
         out_specs=band(planes),
         scratch_shapes=[
             pltpu.VMEM((planes, rows + 16, cols), f32),
             pltpu.VMEM((rows + 16, cols), f32),
-            pltpu.VMEM((levels, 8, cols), f32),
             pltpu.SemaphoreType.DMA((rows // 8,)),
         ],
         compiler_params=pltpu.CompilerParams(
@@ -373,8 +543,8 @@
         cost_estimate=pl.CostEstimate(
             flops=100_000_000, bytes_accessed=40_000_000, transcendentals=0
         ),
-        name="tracer",
-    )(tracers, south, north, west, east, mask_south, mask_north, mask, depth, flow, forcing)
+        name="advect",
+    )(tracers, south, north, west, east, mask_south, mask_north, mask, depth, flow)
 
 
 def baro_kernel(
@@ -383,32 +553,23 @@
     mask_ref,
     depth_ref,
     baro_ref,
-    south_ref,
-    north_ref,
-    west_ref,
-    east_ref,
-    fs_ref,
-    fn_ref,
-    fw_ref,
-    fe_ref,
-    fsw_ref,
-    fse_ref,
-    fnw_ref,
-    fne_ref,
-    height_out,
-    flow_out,
+    *refs,
 ):
     rows, cols = height_ref.shape
+    height_out, flow_out = refs[-2:]
+
+    def widen(k, tile, around):
+        s, n, w, e, sw, se, nw, ne = [a[k] for a in around]
+        low = jnp.concatenate([sw, s, se], 1)
+        mid = jnp.concatenate([w, tile, e], 1)
+        top = jnp.concatenate([nw, n, ne], 1)
+        return jnp.concatenate([low, mid, top], 0)
 
     def still(k, tile):
-        middle = jnp.concatenate([south_ref[k], tile, north_ref[k]], 0)
-        return jnp.concatenate([west_ref[k], middle, east_ref[k]], 1)
+        return widen(k, tile, refs[:8])
 
     def forced(k):
-        low = jnp.concatenate([fsw_ref[k], fs_ref[k], fse_ref[k]], 1)
-        mid = jnp.concatenate([fw_ref[k], baro_ref[k], fe_ref[k]], 1)
-        top = jnp.concatenate([fnw_ref[k], fn_ref[k], fne_ref[k]], 1)
-        return jnp.concatenate([low, mid, top], 0)
+        return widen(k, baro_ref[k], refs[8:16])
 
     height = still(0, height_ref[...])
     along = still(1, flow_ref[0])
@@ -436,8 +597,7 @@
 
 
 def local(
-    ny,
-    nx,
+    mesh_shape,
     atm_flux,
     margin_source,
     margin_cell,
@@ -452,101 +612,58 @@
     levels = tracers.shape[1]
     tile_rows, tile_cols = sea_height.shape
     fields = atm_flux.shape[0]
-    tiles = ny * nx
+    tiles = mesh_shape[0] * mesh_shape[1] * mesh_shape[2]
     cap = 2 * margin_source.shape[0] // tiles
-
-    def from_side(a, dy, dx):
-        perm = [
-            ((y + dy) * nx + x + dx, y * nx + x)
-            for y in range(ny)
-            for x in range(nx)
-            if 0 <= y + dy < ny and 0 <= x + dx < nx
-        ]
-        return lax.ppermute(a, AXES, perm)
+    parts = 2 if cap % 2 == 0 else 1
+    share = cap // parts
+
+    outgoing = pack(
+        margin_tile[:, 0], atm_flux, margin_source, margin_cell, margin_weight, tiles, cap, parts
+    )
+    arrivals = [
+        lax.all_to_all(a, AXES, split_axis=0, concat_axis=0, tiled=True) for a in outgoing
+    ]
 
     flat = tracers.reshape(2 * levels, tile_rows, tile_cols)
     still = jnp.stack(
         [sea_height, transport[0], transport[1], land_mask.astype(f32), sea_depth]
     )
-    count = still.shape[0]
-
-    def lines(edge, band):
-        return jnp.concatenate([edge, band.reshape(count * RIM, tile_cols)], 0)
-
-    planes = 2 * levels
-    got_s = from_side(lines(flat[:, -1], still[:, -RIM:]), -1, 0)
-    got_n = from_side(lines(flat[:, 0], still[:, :RIM]), 1, 0)
-    still_s = got_s[planes:].reshape(count, RIM, tile_cols)
-    still_n = got_n[planes:].reshape(count, RIM, tile_cols)
-    tall = jnp.concatenate([still_s, still, still_n], 1)
-    first, last = edge_columns(flat, land_mask)
-    ext = (tile_rows + 2 * RIM) * count
-
-    def columns(edge, band):
-        return jnp.concatenate([edge, band.reshape(ext, LANES)], 0)
-
-    got_w = from_side(columns(last, tall[:, :, -LANES:]), 0, -1)
-    got_e = from_side(columns(first, tall[:, :, :LANES]), 0, 1)
-    still_w = got_w[tile_rows:].reshape(count, -1, LANES)
-    still_e = got_e[tile_rows:].reshape(count, -1, LANES)
-
-    outgoing = pack(
-        margin_tile[:, 0], atm_flux, margin_source, margin_cell, margin_weight, tiles, cap
+    first, last, bottom, top = tracer_edges(flat, land_mask)
+    *rim, south, north, west, east = exchange(mesh_shape, still, (top, bottom, last, first), 0)
+    moved = advect_step(
+        flat, south, north, west, east, rim[0][3], rim[1][3], land_mask, sea_depth, transport
     )
-    arrived = lax.all_to_all(outgoing, AXES, split_axis=0, concat_axis=0, tiled=True)
-    slot_rows = arrived[:, cap * fields : cap * fields + cap, 0].astype(jnp.int32) // tile_cols
-    forcing, baro = scatter(
-        slot_rows.reshape(-1), arrived, cap, fields, tile_rows, tile_cols
-    )
-
-    low, high = slice(None, RIM), slice(-RIM, None)
-    left, right = slice(None, LANES), slice(-LANES, None)
-    halo = [
-        from_side(baro[:, high], -1, 0),
-        from_side(baro[:, low], 1, 0),
-        from_side(baro[:, :, right], 0, -1),
-        from_side(baro[:, :, left], 0, 1),
-        from_side(baro[:, high, right], -1, -1),
-        from_side(baro[:, high, left], -1, 1),
-        from_side(baro[:, low, right], 1, -1),
-        from_side(baro[:, low, left], 1, 1),
-    ]
-    new_tracers = tracer_step(
-        levels,
-        flat,
-        got_s[:planes],
-        got_n[:planes],
-        got_w[:tile_rows],
-        got_e[:tile_rows],
-        still_s[3],
-        still_n[3],
-        land_mask,
-        sea_depth,
-        transport,
-        forcing,
-    )
+
+    total = None
+    for c, arrived in enumerate(arrivals):
+        cells = arrived[:, share * fields : share * fields + share, 0]
+        slot_rows = cells.astype(jnp.int32) // tile_cols
+        done = scatter(
+            slot_rows.reshape(-1),
+            arrived,
+            total,
+            share,
+            fields,
+            tile_rows,
+            tile_cols,
+            c == parts - 1,
+        )
+        total = done[0]
+    forcing, baro = done
+    halo = exchange(mesh_shape, baro, (), 1)
+    new_tracers = solve_step(levels, moved, land_mask, forcing)
     height, flow = pl.pallas_call(
         baro_kernel,
         out_shape=(
             jax.ShapeDtypeStruct(sea_height.shape, f32),
             jax.ShapeDtypeStruct(transport.shape, f32),
         ),
-        in_specs=[vmem()] * 17,
+        in_specs=[vmem()] * (5 + 2 * len(WAYS)),
         out_specs=(vmem(), vmem()),
         compiler_params=pltpu.CompilerParams(vmem_limit_bytes=VMEM_LIMIT),
+        cost_estimate=pl.CostEstimate(flops=10_000_000, bytes_accessed=8_000_000, transcendentals=0),
         name="baro",
-    )(
-        sea_height,
-        transport,
-        land_mask,
-        sea_depth,
-        baro,
-        still_s,
-        still_n,
-        still_w,
-        still_e,
-        *halo,
-    )
+    )(sea_height, transport, land_mask, sea_depth, baro, *rim, *halo)
     return (height, flow, new_tracers.reshape(tracers.shape))
 
 
@@ -568,7 +685,5 @@
         P(None, ("comp", "ty"), "tx"),
         P(None, None, ("comp", "ty"), "tx"),
     )
-    ny = mesh.shape["comp"] * mesh.shape["ty"]
-    nx = mesh.shape["tx"]
-    body = functools.partial(local, ny, nx)
+    body = functools.partial(local, tuple(mesh.shape[axis] for axis in AXES))
     return jax.shard_map(body, mesh=mesh, in_specs=in_specs, out_specs=out_specs, check_vma=False)

time: 177 us -> 163 us (0.921)
  the two profiles are of different devices: /device:TPU:19 before, /device:TPU:5 now
where the time goes in v1:
time: 163 us; the launch traced here: 161 us
  Pallas kernels  116 us (71%)
  blocking collectives  35.7 us (22%)
  other arithmetic  3.6 us (2%)
  starting transfers between devices  3.59 us (2%)
    pallas_call x2, Pallas kernels, exchange(): pl.pallas_call(functools.partial(exchange_kernel, mesh_shape, len(lines))...  50.4 us
    all_to_all x1, blocking collectives, local(): lax.all_to_all(a, AXES, split_axis=0, concat_axis=0, tiled=True)  35.7 us
    pallas_call x2, Pallas kernels, scatter(): pl.pallas_call(functools.partial(scatter_kernel, cap, fields, tile_rows,...  28.8 us
    pallas_call x1, Pallas kernels, advect_step(): pl.pallas_call(advect_kernel, out_shape=jax.ShapeDtypeStruct(tracers.shap...  11.6 us
    pallas_call x1, Pallas kernels, solve_step(): pl.pallas_call(functools.partial(solve_kernel, levels), out_shape=jax.Sha...  10.5 us
    pallas_call x1, Pallas kernels, pack(): pl.pallas_call(functools.partial(pack_kernel, cap), out_shape=[jax.ShapeD...  6.05 us
    pallas_call x1, Pallas kernels, local(): pl.pallas_call(baro_kernel, out_shape=(jax.ShapeDtypeStruct(sea_height.sh...  4.74 us
    pallas_call x1, Pallas kernels, tracer_edges(): pl.pallas_call(edges_kernel, out_shape=(strip, strip, line, line), grid=(...  3.66 us
  transfers between devices with their start and end apart: 1, of which 0 were waited for; matrix products, arithmetic and copies ran while one was open for 2% of the time, Pallas kernels for 29%

profile of v1, /device:TPU:5, one launch (start us, length us, event | category | flops | bytes accessed | tf_op | source)
XLA Modules:
  0.0 161.0 jit_solution(15496645181058738011)
XLA Ops:
  0.6 6.0 %pack.1 = (f32[32,72,128]{2,1,0:T(8,128)}, f32[32,72,128]{2,1,0:T(8,128)}) custom-call(s32[256]{0:T(256)} %bitcast.19, f32[8,16384]{1,0:T(8,128)} %flux_ref.1, s32[256,128]{1,0:T(8,128)} %src_ref.1, s32[256,128]{1,0:T(8,128)} %cell_ref.1, f32[256,128]{1,0:T(8,128)} %weight_ref.1), custom_call_target="tpu_custom_call" | custom-call | flops 10000000 | bytes 4000000 | tf_op jit(solution)/shard_map/pack/pallas_call | solution.py:85
  6.7 35.7 %all_to_all.10.in_ref = f32[32,72,128]{2,1,0:T(8,128)S(1)} all-to-all(f32[32,72,128]{2,1,0:T(8,128)} %get-tuple-element.34), channel_id=1, replica_groups=mesh['comp'=2,'ty'=4,'tx'=4] {'comp','ty','tx'}, dimensions={0} | all-to-all | bytes 2359296 | tf_op jit(solution)/shard_map/all_to_all | solution.py:624
  42.3 0.0 copy-start.4
  42.3 3.6 %all-to-all-start = ((f32[32,72,128]{2,1,0:T(8,128)}), f32[32,72,128]{2,1,0:T(8,128)S(1)}, u32[]{:S(2)}, u32[]{:S(2)}) async-start(f32[32,72,128]{2,1,0:T(8,128)} %get-tuple-element.33), calls=%async_computation | async-start | bytes 2359296 | tf_op jit(solution)/shard_map/all_to_all | solution.py:624
  45.9 0.0 copy-start
  46.0 0.0 copy-start.1
  46.0 0.0 copy-start.2
  46.0 0.0 copy-start.5
  46.0 3.7 %edges.1 = (f32[64,128]{1,0:T(8,128)}, f32[64,128]{1,0:T(8,128)}, f32[32,1024]{1,0:T(8,128)}, f32[32,1024]{1,0:T(8,128)}) custom-call(f32[32,64,1024]{2,1,0:T(8,128)} %bitcast.11, f32[32,64,1024]{2,1,0:T(8,128)} %bitcast.12, f32[32,64,1024]{2,1,0:T(8,128)} %bitcast.13, f32[32,64,1024]{2,1,0:T(8,128)} %bitcast.14, s32[64,1024]{1,0:T(8,128)} %mask_ref.5, ...), custom_call_target="tpu_custom_call" | custom-call | flops 1000000 | bytes 5000000 | tf_op jit(solution)/shard_map/edges/pallas_call | solution.py:227
  49.7 0.0 copy-done
  49.7 0.0 copy-done.1
  49.7 0.0 copy-done.2
  49.7 0.0 copy-done.5
  49.7 1.2 pad_maximum_fusion.refs_0_
  50.9 31.1 %exchange.2 = (f32[5,8,1024]{2,1,0:T(8,128)}, f32[5,8,1024]{2,1,0:T(8,128)}, f32[5,64,128]{2,1,0:T(8,128)}, f32[5,64,128]{2,1,0:T(8,128)}, f32[5,8,128]{2,1,0:T(...) custom-call(f32[5,64,1024]{2,1,0:T(8,128)} %pad_maximum_fusion.refs_, ...), custom_call_target="tpu_custom_call" | custom-call | flops 1000 | bytes 5000000 | tf_op jit(solution)/shard_map/exchange/pallas_call | solution.py:329
  82.0 1.4 slice_bitcast_fusion
  83.4 11.6 %advect.1.moved_ref = f32[32,64,1024]{2,1,0:T(8,128)} custom-call(f32[32,64,1024]{2,1,0:T(8,128)} %bitcast.15, f32[32,1024]{1,0:T(8,128)} %get-tuple-element.58.south_ref, f32[32,1024]{1,0:T(8,128)} %get-tuple-element.59.north_ref, f32[64,128]{1,0:T(8,128)} %get-tuple-element.60.west_ref, f32[64,128]{1,0:T(8,128)} %get-tuple-element.61.east_ref, ...), custom_call_target="tpu_custom_call" | custom-call | flops 100000000 | bytes 40000000 | tf_op jit(solution)/shard_map/advect/pallas_call | solution.py:518
  95.0 0.0 copy-done.4
  95.0 0.6 fusion
  95.6 0.1 convert_element_type.20
  95.7 0.6 and_select_fusion.row_ref
  96.2 0.0 all-to-all-done.in_ref
  96.3 0.0 copy-start.3
  96.3 0.6 fusion.1
  96.9 0.1 convert_element_type.18
  97.0 0.6 and_select_fusion.1.row_ref
  97.5 13.2 %scatter.2.rest_0_ = f32[4096,128]{1,0:T(8,128)} custom-call(s32[256]{0:T(256)} %and_select_fusion.row_ref, f32[32,72,128]{2,1,0:T(8,128)} %copy-done.4), custom_call_target="tpu_custom_call" | custom-call | flops 2000000000 | bytes 20000000 | tf_op jit(solution)/shard_map/scatter/pallas_call | solution.py:181
  110.8 0.0 copy-done.3
  110.8 15.6 %scatter.3 = (f32[8,64,1024]{2,1,0:T(8,128)}, f32[4,64,1024]{2,1,0:T(8,128)}) custom-call(s32[256]{0:T(256)} %and_select_fusion.1.row_ref, f32[32,72,128]{2,1,0:T(8,128)} %copy-done.3, f32[4096,128]{1,0:T(8,128)} %scatter.2.rest_0_), custom_call_target="tpu_custom_call" | custom-call | flops 2000000000 | bytes 20000000 | tf_op jit(solution)/shard_map/scatter/pallas_call | solution.py:181
  126.3 19.4 %exchange.3 = (f32[4,8,1024]{2,1,0:T(8,128)}, f32[4,8,1024]{2,1,0:T(8,128)}, f32[4,64,128]{2,1,0:T(8,128)}, f32[4,64,128]{2,1,0:T(8,128)}, f32[4,8,128]{2,1,0:T(...) custom-call(f32[4,64,1024]{2,1,0:T(8,128)} %get-tuple-element.35.refs_0_.baro_ref), custom_call_target="tpu_custom_call" | custom-call | flops 1000 | bytes 5000000 | tf_op jit(solution)/shard_map/exchange/pallas_call | solution.py:329
  145.7 10.5 %solve.1 = f32[32,64,1024]{2,1,0:T(8,128)} custom-call(f32[32,64,1024]{2,1,0:T(8,128)} %advect.1.moved_ref, s32[64,1024]{1,0:T(8,128)} %mask_ref.5, f32[8,64,1024]{2,1,0:T(8,128)} %get-tuple-element.62.forcing_ref), custom_call_target="tpu_custom_call" | custom-call | flops 30000000 | bytes 25000000 | tf_op jit(solution)/shard_map/solve/pallas_call | solution.py:488
  156.2 4.7 %baro.1 = (f32[64,1024]{1,0:T(8,128)}, f32[2,64,1024]{2,1,0:T(8,128)}) custom-call(f32[64,1024]{1,0:T(8,128)} %height_ref.1, f32[2,64,1024]{2,1,0:T(8,128)} %flow_ref.3, s32[64,1024]{1,0:T(8,128)} %mask_ref.5, f32[64,1024]{1,0:T(8,128)} %depth_ref.3, f32[4,64,1024]{2,1,0:T(8,128)} %get-tuple-element.35.refs_0_.baro_ref, ...), custom_call_target="tpu_custom_call" | custom-call | flops 10000000 | bytes 8000000 | tf_op jit(solution)/shard_map/baro/pallas_call | solution.py:655
  (1 shorter events, 0.0 us)
Async XLA Ops:
  42.3 52.6 %copy-start.4 = (f32[32,72,128]{2,1,0:T(8,128)}, f32[32,72,128]{2,1,0:T(8,128)S(1)}, u32[]{:S(2)}) copy-start(f32[32,72,128]{2,1,0:T(8,128)S(1)} %all_to_all.10.in_ref) | copy-start | bytes 3538948
  42.3 53.9 %all-to-all-start = ((f32[32,72,128]{2,1,0:T(8,128)}), f32[32,72,128]{2,1,0:T(8,128)S(1)}, u32[]{:S(2)}, u32[]{:S(2)}) async-start(f32[32,72,128]{2,1,0:T(8,128)} %get-tuple-element.33), calls=%async_computation | async-start | bytes 2359296 | tf_op jit(solution)/shard_map/all_to_all | solution.py:624
  45.9 3.7 %copy-start = (s32[64,1024]{1,0:T(8,128)S(1)}, s32[64,1024]{1,0:T(8,128)}, u32[]{:S(2)}) copy-start(s32[64,1024]{1,0:T(8,128)} %mask_ref.5) | copy-start | bytes 786436
  46.0 3.7 %copy-start.1 = (f32[2,64,1024]{2,1,0:T(8,128)S(1)}, f32[2,64,1024]{2,1,0:T(8,128)}, u32[]{:S(2)}) copy-start(f32[2,64,1024]{2,1,0:T(8,128)} %flow_ref.3) | copy-start | bytes 1572868
  46.0 3.7 %copy-start.2 = (f32[64,1024]{1,0:T(8,128)S(1)}, f32[64,1024]{1,0:T(8,128)}, u32[]{:S(2)}) copy-start(f32[64,1024]{1,0:T(8,128)} %depth_ref.3) | copy-start | bytes 786436
  46.0 3.7 %copy-start.5 = (f32[64,1024]{1,0:T(8,128)S(1)}, f32[64,1024]{1,0:T(8,128)}, u32[]{:S(2)}) copy-start(f32[64,1024]{1,0:T(8,128)} %height_ref.1) | copy-start | bytes 786436
  96.3 14.5 %copy-start.3 = (f32[32,72,128]{2,1,0:T(8,128)}, f32[32,72,128]{2,1,0:T(8,128)S(1)}, u32[]{:S(2)}) copy-start(f32[32,72,128]{2,1,0:T(8,128)S(1)} %all-to-all-done.in_ref) | copy-start | bytes 3538948

commit v2 on v1

--- a/solution.py
+++ b/solution.py
@@ -246,15 +246,23 @@
 WAYS = ((1, 0), (-1, 0), (0, 1), (0, -1), (1, 1), (1, -1), (-1, 1), (-1, -1))
 
 
-def exchange_kernel(mesh_shape, extras, *refs):
+def exchange_kernel(mesh_shape, extras, moving, *refs):
     comps, depth, nx = mesh_shape
     ny = comps * depth
+    total = ny * nx
+    refs = list(refs)
+    if moving:
+        outgoing = refs.pop(0)
     band, lines = refs[0], refs[1 : 1 + extras]
     outs = refs[1 + extras : 1 + 2 * extras + len(WAYS)]
+    if moving:
+        arrived = refs[1 + 2 * extras + len(WAYS)]
+        own_sem, out_sems, in_sems = refs[-5:-2]
     send_sems, recv_sems = refs[-2:]
     rows, cols = band.shape[1:]
-    y = lax.axis_index("comp") * depth + lax.axis_index("ty")
-    x = lax.axis_index("tx")
+    c, t, x = [lax.axis_index(axis) for axis in AXES]
+    y = c * depth + t
+    me = y * nx + x
 
     def inside(dy, dx):
         return (y + dy >= 0) & (y + dy < ny) & (x + dx >= 0) & (x + dx < nx)
@@ -262,18 +270,50 @@
     def place(dy, dx):
         return ((y + dy) // depth, (y + dy) % depth, x + dx)
 
+    def partner(d, sign):
+        dt, dc, dx = d % depth, d // depth % comps, d // (depth * comps)
+        if sign < 0:
+            dt, dc, dx = depth - dt, comps - dc, nx - dx
+        return ((c + dc) % comps, (t + dt) % depth, (x + dx) % nx)
+
+    def number(at):
+        return (at[0] * depth + at[1]) * nx + at[2]
+
+    def shift(d):
+        return pltpu.make_async_remote_copy(
+            src_ref=outgoing.at[number(partner(d, 1))],
+            dst_ref=arrived.at[me],
+            send_sem=out_sems.at[d],
+            recv_sem=in_sems.at[d],
+            device_id=partner(d, 1),
+            device_id_type=pl.DeviceIdType.MESH,
+        )
+
     barrier = pltpu.get_barrier_semaphore()
-    near = jnp.int32(0)
-    for way in WAYS:
-        near = near + inside(*way).astype(jnp.int32)
-
-        @pl.when(inside(*way))
-        def _(way=way):
+    if moving:
+        own = pltpu.make_async_copy(outgoing.at[me], arrived.at[me], own_sem)
+        own.start()
+
+        def greet(d, carry):
             pl.semaphore_signal(
-                barrier, inc=1, device_id=place(*way), device_id_type=pl.DeviceIdType.MESH
+                barrier, inc=1, device_id=partner(d, 1), device_id_type=pl.DeviceIdType.MESH
             )
-
-    pl.semaphore_wait(barrier, near)
+            return carry
+
+        lax.fori_loop(1, total, greet, 0)
+        pl.semaphore_wait(barrier, total - 1)
+    else:
+        near = jnp.int32(0)
+        for way in WAYS:
+            near = near + inside(*way).astype(jnp.int32)
+
+            @pl.when(inside(*way))
+            def _(way=way):
+                pl.semaphore_signal(
+                    barrier, inc=1, device_id=place(*way), device_id_type=pl.DeviceIdType.MESH
+                )
+
+        pl.semaphore_wait(barrier, near)
 
     def pieces():
         for k, (dy, dx) in enumerate(WAYS):
@@ -310,6 +350,13 @@
             dst[...] = jnp.zeros(dst.shape, f32)
 
         copies.append((copy, sends, gets))
+    if moving:
+
+        def start(d, carry):
+            shift(d).start()
+            return carry
+
+        lax.fori_loop(1, total, start, 0)
     for copy, sends, gets in copies:
 
         @pl.when(sends)
@@ -320,30 +367,59 @@
         def _(copy=copy):
             copy().wait_recv()
 
-
-def exchange(mesh_shape, band, lines, number):
+    if moving:
+
+        def finish(d, carry):
+            shift(d).wait_send()
+            came = partner(d, -1)
+            pltpu.make_async_remote_copy(
+                src_ref=outgoing.at[number(came)],
+                dst_ref=arrived.at[number(came)],
+                send_sem=out_sems.at[d],
+                recv_sem=in_sems.at[d],
+                device_id=came,
+                device_id_type=pl.DeviceIdType.MESH,
+            ).wait_recv()
+            return carry
+
+        lax.fori_loop(1, total, finish, 0)
+        own.wait()
+
+
+def exchange(mesh_shape, band, lines, number, outgoing=None):
     count, rows, cols = band.shape
+    moving = outgoing is not None
     shapes = [
         (count, RIM if dy else rows, LANES if dx else cols) for dy, dx in WAYS
     ] + [a.shape for a in lines]
+    pieces = len(shapes)
+    first, sems = [], []
+    if moving:
+        first = [outgoing]
+        shapes.append(outgoing.shape)
+        total = outgoing.shape[0]
+        sems = [
+            pltpu.SemaphoreType.DMA,
+            pltpu.SemaphoreType.DMA((total,)),
+            pltpu.SemaphoreType.DMA((total,)),
+        ]
     return pl.pallas_call(
-        functools.partial(exchange_kernel, mesh_shape, len(lines)),
+        functools.partial(exchange_kernel, mesh_shape, len(lines), moving),
         out_shape=[jax.ShapeDtypeStruct(s, f32) for s in shapes],
-        in_specs=[vmem()] * (1 + len(lines)),
+        in_specs=[vmem()] * (len(first) + 1 + len(lines)),
         out_specs=[vmem()] * len(shapes),
-        scratch_shapes=[
-            pltpu.SemaphoreType.DMA((len(shapes),)),
-            pltpu.SemaphoreType.DMA((len(shapes),)),
-        ],
+        scratch_shapes=sems
+        + [pltpu.SemaphoreType.DMA((pieces,)), pltpu.SemaphoreType.DMA((pieces,))],
         compiler_params=pltpu.CompilerParams(
             collective_id=number, has_side_effects=True, vmem_limit_bytes=VMEM_LIMIT
         ),
         cost_estimate=pl.CostEstimate(flops=1000, bytes_accessed=5_000_000, transcendentals=0),
-        name="exchange",
-    )(band, *lines)
-
-
-def advect_kernel(
+        name="move" if moving else "exchange",
+    )(*first, band, *lines)
+
+
+def tracer_kernel(
+    levels,
     tracer_hbm,
     south_ref,
     north_ref,
@@ -354,9 +430,11 @@
     mask_ref,
     depth_ref,
     flow_ref,
+    forcing_ref,
     out_ref,
     held,
     mask_held,
+    ratio_ref,
     sems,
 ):
     planes = held.shape[0]
@@ -425,29 +503,16 @@
     cs = mask_s * (diffuse + advect * jnp.maximum(v, 0.0))
     c0 = 1.0 - (ce + cw + cn + cs)
 
-    ocean = mask > 0.5
-    for p in range(planes):
-        q = held[p, here, :]
-        qe, qw, qn, qs = sides(
-            q, held[p, pl.ds(base + 7, 1), :], held[p, pl.ds(base + 16, 1), :], p
-        )
-        moved = c0 * q + ce * qe + cw * qw + cn * qn + cs * qs
-        out_ref[p] = jnp.where(ocean, moved, q)
-
-
-def solve_kernel(levels, moved_ref, mask_ref, forcing_ref, out_ref, ratio_ref):
     depths = np.arange(levels, dtype=np.float32)
     absorb = np.exp(-depths / np.float32(3)) - np.exp(-(depths + 1) / np.float32(3))
     fade = np.exp(-depths / np.float32(2))
-    ocean = mask_ref[...].astype(f32)
-    floor = 0.2 * ocean
-    stir = (0.5 * ocean) * forcing_ref[7] * forcing_ref[7]
-    sun = (0.5 * ocean) * forcing_ref[4]
+    stir = 0.5 * forcing_ref[7] * forcing_ref[7]
+    sun = 0.5 * forcing_ref[4]
     ratio = None
     last = [None, None]
     lower = None
     for k in range(levels):
-        upper = floor + stir * float(fade[k]) if k < levels - 1 else None
+        upper = 0.2 + stir * float(fade[k]) if k < levels - 1 else None
         pivot = 1.0
         if upper is not None:
             pivot = pivot + upper
@@ -459,64 +524,46 @@
             ratio_ref[k] = ratio
         for t in range(2):
             p = t * levels + k
-            side = moved_ref[p]
+            q = held[p, here, :]
+            qe, qw, qn, qs = sides(
+                q, held[p, pl.ds(base + 7, 1), :], held[p, pl.ds(base + 16, 1), :], p
+            )
+            side = c0 * q + ce * qe + cw * qw + cn * qn + cs * qs
             if t == 0:
                 side = side + sun * float(absorb[k])
                 if k == 0:
-                    side = side + (0.5 * ocean) * forcing_ref[3]
+                    side = side + 0.5 * forcing_ref[3]
             elif k == 0:
-                side = side + ocean * (0.5 * forcing_ref[5] - 0.3 * forcing_ref[6])
+                side = side + (0.5 * forcing_ref[5] - 0.3 * forcing_ref[6])
             if lower is not None:
                 side = side + lower * last[t]
             last[t] = side * scale
             out_ref[p] = last[t]
         lower = upper
-    for k in range(levels - 2, -1, -1):
+    ocean = mask > 0.5
+    for k in range(levels - 1, -1, -1):
         for t in range(2):
             p = t * levels + k
-            last[t] = out_ref[p] - ratio_ref[k] * last[t]
-            out_ref[p] = last[t]
-
-
-def solve_step(levels, moved, mask, forcing):
-    planes, rows, cols = moved.shape
+            if k < levels - 1:
+                last[t] = out_ref[p] - ratio_ref[k] * last[t]
+            out_ref[p] = jnp.where(ocean, last[t], held[p, here, :])
+
+
+def tracer_step(
+    levels, tracers, south, north, west, east, mask_south, mask_north, mask, depth, flow, forcing
+):
+    planes, rows, cols = tracers.shape
 
     def band(*lead):
         zeros = (0,) * len(lead)
         return pl.BlockSpec((*lead, 8, cols), lambda i: (*zeros, i, 0))
 
-    return pl.pallas_call(
-        functools.partial(solve_kernel, levels),
-        out_shape=jax.ShapeDtypeStruct(moved.shape, f32),
-        grid=(rows // 8,),
-        in_specs=[band(planes), band(), band(forcing.shape[0])],
-        out_specs=band(planes),
-        scratch_shapes=[pltpu.VMEM((levels, 8, cols), f32)],
-        compiler_params=pltpu.CompilerParams(
-            vmem_limit_bytes=VMEM_LIMIT, dimension_semantics=("arbitrary",)
-        ),
-        cost_estimate=pl.CostEstimate(
-            flops=30_000_000, bytes_accessed=25_000_000, transcendentals=0
-        ),
-        name="solve",
-    )(moved, mask, forcing)
-
-
-def advect_step(
-    tracers, south, north, west, east, mask_south, mask_north, mask, depth, flow
-):
-    planes, rows, cols = tracers.shape
-
-    def band(*lead):
-        zeros = (0,) * len(lead)
-        return pl.BlockSpec((*lead, 8, cols), lambda i: (*zeros, i, 0))
-
     def full(a):
         zeros = (0,) * a.ndim
         return pl.BlockSpec(a.shape, lambda i: zeros)
 
     return pl.pallas_call(
-        advect_kernel,
+        functools.partial(tracer_kernel, levels),
         out_shape=jax.ShapeDtypeStruct(tracers.shape, f32),
         grid=(rows // 8,),
         in_specs=[
@@ -530,11 +577,13 @@
             full(mask),
             band(),
             band(2),
+            band(forcing.shape[0]),
         ],
         out_specs=band(planes),
         scratch_shapes=[
             pltpu.VMEM((planes, rows + 16, cols), f32),
             pltpu.VMEM((rows + 16, cols), f32),
+            pltpu.VMEM((levels, 8, cols), f32),
             pltpu.SemaphoreType.DMA((rows // 8,)),
         ],
         compiler_params=pltpu.CompilerParams(
@@ -543,8 +592,8 @@
         cost_estimate=pl.CostEstimate(
             flops=100_000_000, bytes_accessed=40_000_000, transcendentals=0
         ),
-        name="advect",
-    )(tracers, south, north, west, east, mask_south, mask_north, mask, depth, flow)
+        name="tracer",
+    )(tracers, south, north, west, east, mask_south, mask_north, mask, depth, flow, forcing)
 
 
 def baro_kernel(
@@ -614,28 +663,23 @@
     fields = atm_flux.shape[0]
     tiles = mesh_shape[0] * mesh_shape[1] * mesh_shape[2]
     cap = 2 * margin_source.shape[0] // tiles
-    parts = 2 if cap % 2 == 0 else 1
+    parts = 1
     share = cap // parts
 
     outgoing = pack(
         margin_tile[:, 0], atm_flux, margin_source, margin_cell, margin_weight, tiles, cap, parts
     )
-    arrivals = [
-        lax.all_to_all(a, AXES, split_axis=0, concat_axis=0, tiled=True) for a in outgoing
-    ]
 
     flat = tracers.reshape(2 * levels, tile_rows, tile_cols)
     still = jnp.stack(
         [sea_height, transport[0], transport[1], land_mask.astype(f32), sea_depth]
     )
     first, last, bottom, top = tracer_edges(flat, land_mask)
-    *rim, south, north, west, east = exchange(mesh_shape, still, (top, bottom, last, first), 0)
-    moved = advect_step(
-        flat, south, north, west, east, rim[0][3], rim[1][3], land_mask, sea_depth, transport
+    *rim, south, north, west, east, arrived = exchange(
+        mesh_shape, still, (top, bottom, last, first), 0, outgoing[0]
     )
-
     total = None
-    for c, arrived in enumerate(arrivals):
+    for c, arrived in enumerate([arrived]):
         cells = arrived[:, share * fields : share * fields + share, 0]
         slot_rows = cells.astype(jnp.int32) // tile_cols
         done = scatter(
@@ -651,7 +695,20 @@
         total = done[0]
     forcing, baro = done
     halo = exchange(mesh_shape, baro, (), 1)
-    new_tracers = solve_step(levels, moved, land_mask, forcing)
+    new_tracers = tracer_step(
+        levels,
+        flat,
+        south,
+        north,
+        west,
+        east,
+        rim[0][3],
+        rim[1][3],
+        land_mask,
+        sea_depth,
+        transport,
+        forcing,
+    )
     height, flow = pl.pallas_call(
         baro_kernel,
         out_shape=(

time: 163 us -> 148 us (0.908)
  blocking collectives: 35.7 us -> 0 us
  Pallas kernels: 116 us -> 140 us
  starting transfers between devices: 3.59 us -> 0 us
    all_to_all x1 -> x0, blocking collectives: 35.7 us -> none  [local(): lax.all_to_all(a, AXES, split_axis=0, concat_axis=0, tiled=True)]
    pallas_call x4 -> x3, Pallas kernels: 72.5 us -> 105 us  [the longest x2 90.3 us: exchange(): pl.pallas_call(functools.partial(exchange_kernel, mesh_shape, len(lines),...]
    pallas_call x2 -> x1, Pallas kernels: 28.8 us -> 21.1 us  [scatter(): pl.pallas_call(functools.partial(scatter_kernel, cap, fields, tile_rows,...]
    all_to_all x1 -> x0, starting transfers between devices: 3.59 us -> none  [local(): lax.all_to_all(a, AXES, split_axis=0, concat_axis=0, tiled=True)]
  transfers between devices with their start and end apart: 1 -> 0, of which waited for: 0 -> 0; matrix products, arithmetic and copies ran while one was open for 2% -> 0% of each run, Pallas kernels for 29% -> 0%
where the time goes in v2:
time: 148 us; the launch traced here: 147 us
  Pallas kernels  140 us (95%)
  other arithmetic  4.31 us (3%)
  local copies, waits for them, and re-layouts  1.53 us (1%)
    pallas_call x2, Pallas kernels, exchange(): pl.pallas_call(functools.partial(exchange_kernel, mesh_shape, len(lines),...  90.3 us
    pallas_call x1, Pallas kernels, scatter(): pl.pallas_call(functools.partial(scatter_kernel, cap, fields, tile_rows,...  21.1 us
    pallas_call x1, Pallas kernels, tracer_step(): pl.pallas_call(functools.partial(tracer_kernel, levels), out_shape=jax.Sh...  14.3 us
    pallas_call x1, Pallas kernels, pack(): pl.pallas_call(functools.partial(pack_kernel, cap), out_shape=[jax.ShapeD...  5.91 us
    pallas_call x1, Pallas kernels, local(): pl.pallas_call(baro_kernel, out_shape=(jax.ShapeDtypeStruct(sea_height.sh...  4.75 us
    pallas_call x1, Pallas kernels, tracer_edges(): pl.pallas_call(edges_kernel, out_shape=(strip, strip, line, line), grid=(...  3.65 us

profile of v2, /device:TPU:5, one launch (start us, length us, event | category | flops | bytes accessed | tf_op | source)
XLA Modules:
  0.0 146.7 jit_solution(12129696544876785922)
XLA Ops:
  0.6 1.0 convert_bitcast_fusion
  1.6 0.0 copy-start
  1.6 0.0 copy-start.1
  1.6 0.0 copy-start.2
  1.6 3.6 %edges.1 = (f32[64,128]{1,0:T(8,128)}, f32[64,128]{1,0:T(8,128)}, f32[32,1024]{1,0:T(8,128)}, f32[32,1024]{1,0:T(8,128)}) custom-call(f32[32,64,1024]{2,1,0:T(8,128)} %bitcast.11, f32[32,64,1024]{2,1,0:T(8,128)} %bitcast.12, f32[32,64,1024]{2,1,0:T(8,128)} %bitcast.13, f32[32,64,1024]{2,1,0:T(8,128)} %bitcast.14, s32[64,1024]{1,0:T(8,128)} %mask_ref.3, ...), custom_call_target="tpu_custom_call" | custom-call | flops 1000000 | bytes 5000000 | tf_op jit(solution)/shard_map/edges/pallas_call | solution.py:227
  5.3 0.0 copy-done
  5.3 0.0 copy-done.1
  5.3 0.0 copy-done.2
  5.3 1.2 pad_maximum_fusion.refs_1_
  6.5 5.9 %pack.1.refs_0_ = f32[32,144,128]{2,1,0:T(8,128)} custom-call(s32[256]{0:T(256)} %bitcast.19, f32[8,16384]{1,0:T(8,128)} %flux_ref.1, s32[256,128]{1,0:T(8,128)} %src_ref.1, s32[256,128]{1,0:T(8,128)} %cell_ref.1, f32[256,128]{1,0:T(8,128)} %weight_ref.1), custom_call_target="tpu_custom_call" | custom-call | flops 10000000 | bytes 4000000 | tf_op jit(solution)/shard_map/pack/pallas_call | solution.py:85
  12.4 75.8 %move.1 = (f32[5,8,1024]{2,1,0:T(8,128)}, f32[5,8,1024]{2,1,0:T(8,128)}, f32[5,64,128]{2,1,0:T(8,128)}, f32[5,64,128]{2,1,0:T(8,128)}, f32[5,8,128]{2,1,0:T(8,12...) custom-call(f32[32,144,128]{2,1,0:T(8,128)} %pack.1.refs_0_, ...), custom_call_target="tpu_custom_call" | custom-call | flops 1000 | bytes 5000000 | tf_op jit(solution)/shard_map/move/pallas_call | solution.py:406
  88.2 1.6 %convert_reduce_fusion = s32[32,16]{1,0:T(8,128)S(1)} fusion(f32[32,144,128]{2,1,0:T(8,128)} %get-tuple-element.36.in_ref), kind=kLoop, calls=%fused_computation.1 | loop fusion | flops 512 | bytes 4096 | tf_op jit(solution)/shard_map/convert_element_type | solution.py:684
  89.7 0.1 convert_element_type.12
  89.8 0.6 add_select_fusion.row_ref
  90.4 1.4 slice_bitcast_fusion
  91.9 21.1 %scatter.1 = (f32[8,64,1024]{2,1,0:T(8,128)}, f32[4,64,1024]{2,1,0:T(8,128)}) custom-call(s32[512]{0:T(512)} %add_select_fusion.row_ref, f32[32,144,128]{2,1,0:T(8,128)} %get-tuple-element.36.in_ref), custom_call_target="tpu_custom_call" | custom-call | flops 2000000000 | bytes 20000000 | tf_op jit(solution)/shard_map/scatter/pallas_call | solution.py:181
  113.0 14.6 %exchange.1 = (f32[4,8,1024]{2,1,0:T(8,128)}, f32[4,8,1024]{2,1,0:T(8,128)}, f32[4,64,128]{2,1,0:T(8,128)}, f32[4,64,128]{2,1,0:T(8,128)}, f32[4,8,128]{2,1,0:T(...) custom-call(f32[4,64,1024]{2,1,0:T(8,128)} %get-tuple-element.37.refs_0_.baro_ref), custom_call_target="tpu_custom_call" | custom-call | flops 1000 | bytes 5000000 | tf_op jit(solution)/shard_map/exchange/pallas_call | solution.py:406
  127.6 4.8 %baro.1 = (f32[64,1024]{1,0:T(8,128)}, f32[2,64,1024]{2,1,0:T(8,128)}) custom-call(f32[64,1024]{1,0:T(8,128)} %height_ref.1, f32[2,64,1024]{2,1,0:T(8,128)} %flow_ref.3, s32[64,1024]{1,0:T(8,128)} %mask_ref.3, f32[64,1024]{1,0:T(8,128)} %depth_ref.3, f32[4,64,1024]{2,1,0:T(8,128)} %get-tuple-element.37.refs_0_.baro_ref, ...), custom_call_target="tpu_custom_call" | custom-call | flops 10000000 | bytes 8000000 | tf_op jit(solution)/shard_map/baro/pallas_call | solution.py:712
  132.3 14.3 %tracer.1 = f32[32,64,1024]{2,1,0:T(8,128)} custom-call(f32[32,64,1024]{2,1,0:T(8,128)} %bitcast.15, f32[32,1024]{1,0:T(8,128)} %get-tuple-element.56.south_ref, f32[32,1024]{1,0:T(8,128)} %get-tuple-element.57.north_ref, f32[64,128]{1,0:T(8,128)} %get-tuple-element.58.west_ref, f32[64,128]{1,0:T(8,128)} %get-tuple-element.59.east_ref, ...), custom_call_target="tpu_custom_call" | custom-call | flops 100000000 | bytes 40000000 | tf_op jit(solution)/shard_map/tracer/pallas_call | solution.py:565
Async XLA Ops:
  1.6 3.7 %copy-start = (f32[2,64,1024]{2,1,0:T(8,128)S(1)}, f32[2,64,1024]{2,1,0:T(8,128)}, u32[]{:S(2)}) copy-start(f32[2,64,1024]{2,1,0:T(8,128)} %flow_ref.3) | copy-start | bytes 1572868
  1.6 3.7 %copy-start.1 = (f32[64,1024]{1,0:T(8,128)S(1)}, f32[64,1024]{1,0:T(8,128)}, u32[]{:S(2)}) copy-start(f32[64,1024]{1,0:T(8,128)} %depth_ref.3) | copy-start | bytes 786436
  1.6 3.7 %copy-start.2 = (f32[64,1024]{1,0:T(8,128)S(1)}, f32[64,1024]{1,0:T(8,128)}, u32[]{:S(2)}) copy-start(f32[64,1024]{1,0:T(8,128)} %height_ref.1) | copy-start | bytes 786436

commit v3 on v0

v3 whole, which is shorter than its diff:
```python
import functools

import jax
import jax.numpy as jnp
import numpy as np
from jax import lax
from jax.experimental import pallas as pl
from jax.experimental.pallas import tpu as pltpu
from jax.sharding import PartitionSpec as P

SUB = 3
RIM = 8
LANES = 128
AXES = ("comp", "ty", "tx")

damping = 0.95
advect = 0.15
diffuse = 0.1

f32 = jnp.float32
VMEM_LIMIT = 56 * 1024 * 1024


def vmem():
    return pl.BlockSpec(memory_space=pltpu.VMEM)


def smem():
    return pl.BlockSpec(memory_space=pltpu.SMEM)


def pack_kernel(cap, tile_ref, flux_ref, src_ref, cell_ref, weight_ref, *rest):
    *parts, out_ref, count_ref = rest
    tiles = parts[0].shape[0]
    share = cap // len(parts)
    blocks = src_ref.shape[0]
    fields = flux_ref.shape[0]
    width = src_ref.shape[1]

    def clear(t, carry):
        for c in range(len(parts)):
            out_ref[c * tiles + t] = jnp.zeros(out_ref.shape[1:], f32)
        count_ref[t] = 0
        return carry

    lax.fori_loop(0, tiles, clear, 0)

    def group(g, carry):
        base = pl.multiple_of(g * 8, 8)
        sources = src_ref[pl.ds(base, 8), :]
        cells = cell_ref[pl.ds(base, 8), :].astype(f32)
        weights = weight_ref[pl.ds(base, 8), :]
        for w in range(4):
            start = pl.multiple_of((g * 4 + w) * width, width)
            window = flux_ref[:, pl.ds(start, width)]
            for half in range(2):
                j = 2 * w + half
                index = jnp.broadcast_to(sources[j : j + 1], (fields, width))
                picked = jnp.take_along_axis(window, index, axis=1)
                t = tile_ref[base + j]
                r = count_ref[t]
                count_ref[t] = r + 1
                slot = r % share
                lead = (r // share) * tiles + t
                at = pl.multiple_of(slot * fields, fields)
                out_ref[lead, pl.ds(at, fields), :] = picked * weights[j : j + 1]
                out_ref[lead, pl.ds(share * fields + slot, 1), :] = cells[j : j + 1]
        return carry

    lax.fori_loop(0, blocks // 8, group, 0)
    for c, part in enumerate(parts):

        def move(t, carry, c=c, part=part):
            part[t] = out_ref[c * tiles + t]
            return carry

        lax.fori_loop(0, tiles, move, 0)


def pack(margin_tile, atm_flux, margin_source, margin_cell, margin_weight, tiles, cap, parts):
    fields = atm_flux.shape[0]
    share = cap // parts
    rows = share * fields + -(-share // 8) * 8
    width = margin_source.shape[1]
    return pl.pallas_call(
        functools.partial(pack_kernel, cap),
        out_shape=[jax.ShapeDtypeStruct((tiles, rows, width), f32)] * parts,
        in_specs=[smem(), vmem(), vmem(), vmem(), vmem()],
        out_specs=[vmem()] * parts,
        scratch_shapes=[
            pltpu.VMEM((parts * tiles, rows, width), f32),
            pltpu.SMEM((tiles,), jnp.int32),
        ],
        compiler_params=pltpu.CompilerParams(vmem_limit_bytes=VMEM_LIMIT),
        cost_estimate=pl.CostEstimate(flops=10_000_000, bytes_accessed=4_000_000, transcendentals=0),
        name="pack",
    )(margin_tile, atm_flux, margin_source, margin_cell, margin_weight)


WAYS = ((1, 0), (-1, 0), (0, 1), (0, -1), (1, 1), (1, -1), (-1, 1), (-1, -1))


class Grid:
    def __init__(self, mesh_shape):
        self.comps, self.depth, self.nx = mesh_shape
        self.ny = self.comps * self.depth
        self.total = self.ny * self.nx
        self.c, self.t, self.x = [lax.axis_index(axis) for axis in AXES]
        self.y = self.c * self.depth + self.t

    def inside(self, dy, dx):
        y, x = self.y + dy, self.x + dx
        return (y >= 0) & (y < self.ny) & (x >= 0) & (x < self.nx)

    def place(self, dy, dx):
        return ((self.y + dy) // self.depth, (self.y + dy) % self.depth, self.x + dx)

    def partner(self, d, sign):
        dt, dc = d % self.depth, d // self.depth % self.comps
        dx = d // (self.depth * self.comps)
        if sign < 0:
            dt, dc, dx = self.depth - dt, self.comps - dc, self.nx - dx
        return (
            (self.c + dc) % self.comps,
            (self.t + dt) % self.depth,
            (self.x + dx) % self.nx,
        )

    def number(self, at):
        return (at[0] * self.depth + at[1]) * self.nx + at[2]


def greet_near(grid):
    barrier = pltpu.get_barrier_semaphore()
    near = jnp.int32(0)
    for way in WAYS:
        near = near + grid.inside(*way).astype(jnp.int32)

        @pl.when(grid.inside(*way))
        def _(way=way):
            pl.semaphore_signal(
                barrier, inc=1, device_id=grid.place(*way), device_id_type=pl.DeviceIdType.MESH
            )

    pl.semaphore_wait(barrier, near)


class Halo:
    def __init__(self, grid, band, lines, outs, send_sems, recv_sems):
        rows, cols = band.shape[1:]
        self.copies = []
        for k in range(len(WAYS) + len(lines)):
            way = WAYS[k % len(WAYS)]
            if k < len(WAYS):
                dy, dx = way
                ys = pl.ds(rows - RIM if dy == 1 else 0, RIM if dy else rows)
                xs = pl.ds(cols - LANES if dx == 1 else 0, LANES if dx else cols)
                src = band.at[:, ys, xs]
            else:
                src = lines[k - len(WAYS)]

            def copy(way=way, src=src, k=k):
                return pltpu.make_async_remote_copy(
                    src_ref=src,
                    dst_ref=outs[k],
                    send_sem=send_sems.at[k],
                    recv_sem=recv_sems.at[k],
                    device_id=grid.place(*way),
                    device_id_type=pl.DeviceIdType.MESH,
                )

            gets = grid.inside(-way[0], -way[1])
            self.copies.append((copy, outs[k], grid.inside(*way), gets))

    def start(self):
        for copy, dst, sends, gets in self.copies:

            @pl.when(sends)
            def _(copy=copy):
                copy().start()

            @pl.when(jnp.logical_not(gets))
            def _(dst=dst):
                dst[...] = jnp.zeros(dst.shape, f32)

    def wait(self):
        for copy, _, sends, gets in self.copies:

            @pl.when(sends)
            def _(copy=copy):
                copy().wait_send()

            @pl.when(gets)
            def _(copy=copy):
                copy().wait_recv()


def halo_shapes(count, rows, cols):
    return [(count, RIM if dy else rows, LANES if dx else cols) for dy, dx in WAYS]


def move_kernel(
    mesh_shape,
    cap,
    outgoing,
    tracer_hbm,
    mask_ref,
    height_ref,
    flow_ref,
    depth_ref,
    *refs,
):
    grid = Grid(mesh_shape)
    count = len(WAYS) + 4
    outs = refs[:count]
    forcing_ref, baro_ref = refs[count : count + 2]
    (
        arrived,
        band,
        west_blk,
        east_blk,
        low_blk,
        high_blk,
        top,
        bottom,
        last,
        first,
        spread,
        row_ref,
        own_sem,
        load_sems,
        out_sems,
        in_sems,
        send_sems,
        recv_sems,
    ) = refs[count + 2 :]
    fields, rows, cols = forcing_ref.shape
    planes = west_blk.shape[0]
    width = arrived.shape[2]
    highs = cols // LANES
    lines = highs * fields
    slots = row_ref.shape[0]
    owners = slots // cap
    total = grid.total
    me = grid.number((grid.c, grid.t, grid.x))

    def shift(d):
        to = grid.partner(d, 1)
        return pltpu.make_async_remote_copy(
            src_ref=outgoing.at[grid.number(to)],
            dst_ref=arrived.at[me],
            send_sem=out_sems.at[d],
            recv_sem=in_sems.at[d],
            device_id=to,
            device_id_type=pl.DeviceIdType.MESH,
        )

    own = pltpu.make_async_copy(outgoing.at[me], arrived.at[me], own_sem)
    own.start()
    loads = [
        pltpu.make_async_copy(src, dst, load_sems.at[k])
        for k, (src, dst) in enumerate(
            (
                (tracer_hbm.at[:, :, pl.ds(0, LANES)], west_blk),
                (tracer_hbm.at[:, :, pl.ds(cols - LANES, LANES)], east_blk),
                (tracer_hbm.at[:, pl.ds(0, 8), :], low_blk),
                (tracer_hbm.at[:, pl.ds(rows - 8, 8), :], high_blk),
            )
        )
    ]
    for load in loads:
        load.start()

    barrier = pltpu.get_barrier_semaphore()

    def greet(d, carry):
        pl.semaphore_signal(
            barrier, inc=1, device_id=grid.partner(d, 1), device_id_type=pl.DeviceIdType.MESH
        )
        return carry

    lax.fori_loop(1, total, greet, 0)
    pl.semaphore_wait(barrier, total - 1)

    def start(d, carry):
        shift(d).start()
        return carry

    lax.fori_loop(1, total, start, 0)

    band[0] = height_ref[...]
    band[1] = flow_ref[0]
    band[2] = flow_ref[1]
    band[3] = mask_ref[...].astype(f32)
    band[4] = depth_ref[...]
    for load in loads:
        load.wait()
    lane = lax.broadcasted_iota(jnp.int32, (rows, LANES), 1)
    for src, dst, col, side in (
        (west_blk, first, 0, 0),
        (east_blk, last, LANES - 1, cols - LANES),
    ):
        edge = band[3, :, side : side + LANES][:, col : col + 1]
        values = jnp.where(lane == planes, jnp.broadcast_to(edge, (rows, LANES)), 0.0)
        for p in range(planes):
            column = src[p, :, col : col + 1]
            values = jnp.where(lane == p, jnp.broadcast_to(column, (rows, LANES)), values)
        dst[...] = values
    for p in range(planes):
        bottom[p : p + 1, :] = low_blk[p, 0:1, :]
        top[p : p + 1, :] = high_blk[p, 7:8, :]
    halo = Halo(grid, band, (top, bottom, last, first), outs, send_sems, recv_sems)
    halo.start()

    forcing_ref[...] = jnp.zeros(forcing_ref.shape, f32)
    low_iota = lax.broadcasted_iota(jnp.int32, (LANES, width), 0)
    lane_iota = lax.broadcasted_iota(jnp.int32, (1, LANES), 1)
    unroll = 4 if cap % 4 == 0 else 1

    def group_step(g, carry):
        def owner_step(n, carry):
            d = g * owners + n
            came = grid.partner(d, -1)
            source = grid.number(came)

            @pl.when(d == 0)
            def _():
                own.wait()

            @pl.when(d > 0)
            def _():
                pltpu.make_async_remote_copy(
                    src_ref=outgoing.at[source],
                    dst_ref=arrived.at[source],
                    send_sem=out_sems.at[d],
                    recv_sem=in_sems.at[d],
                    device_id=came,
                    device_id_type=pl.DeviceIdType.MESH,
                ).wait_recv()

            def slot_step(rb, carry):
                for ru in range(unroll):
                    r = rb * unroll + ru
                    cell = arrived[source, pl.ds(cap * fields + r, 1), :].astype(jnp.int32)
                    row = lax.div(cell, jnp.full_like(cell, cols))
                    col = cell - row * cols
                    high = jnp.broadcast_to(col // LANES, (fields, width))
                    low = jnp.broadcast_to(col % LANES, (LANES, width))
                    onehot = jnp.where(low_iota == low, 1.0, 0.0).astype(jnp.bfloat16)
                    at = pl.multiple_of(r * fields, fields)
                    values = arrived[source, pl.ds(at, fields), :]
                    coarse = values.astype(jnp.bfloat16).astype(f32)
                    fine = values - coarse
                    picks = [high == h for h in range(highs)]
                    left = jnp.concatenate(
                        [jnp.where(p, coarse, 0.0) for p in picks]
                        + [jnp.where(p, fine, 0.0) for p in picks],
                        axis=0,
                    ).astype(jnp.bfloat16)
                    both = lax.dot_general(
                        left, onehot, (((1,), (1,)), ((), ())), preferred_element_type=f32
                    )
                    slot = n * cap + r
                    spread[pl.ds(slot, lines, stride=slots), :] = both[:lines] + both[lines:]
                    hit = jnp.broadcast_to(row[:, 0:1], (1, LANES)) == lane_iota
                    row_ref[pl.ds(slot, 1), :] = jnp.where(hit, 1.0, 0.0)
                return carry

            lax.fori_loop(0, cap // unroll, slot_step, 0)
            return carry

        lax.fori_loop(0, owners, owner_step, 0)
        onto = row_ref[...].T[:rows].astype(jnp.bfloat16)

        def field_step(f, carry):
            for h in range(highs):
                base = pl.multiple_of((h * fields + f) * slots, slots)
                values = spread[pl.ds(base, slots), :]
                coarse = values.astype(jnp.bfloat16)
                fine = (values - coarse.astype(f32)).astype(jnp.bfloat16)
                part = jnp.dot(onto, coarse, preferred_element_type=f32)
                part = part + jnp.dot(onto, fine, preferred_element_type=f32)
                cs = slice(h * LANES, (h + 1) * LANES)
                forcing_ref[f, :, cs] = forcing_ref[f, :, cs] + part
            return carry

        lax.fori_loop(0, fields, field_step, 0)
        return carry

    lax.fori_loop(0, total // owners, group_step, 0)
    baro_ref[0] = 0.5 * forcing_ref[2]
    baro_ref[1] = 0.5 * forcing_ref[0]
    baro_ref[2] = 0.5 * forcing_ref[1]
    baro_ref[3] = 0.1 * (forcing_ref[6] - forcing_ref[5])

    halo.wait()

    def finish(d, carry):
        shift(d).wait_send()
        return carry

    lax.fori_loop(1, total, finish, 0)


def move(mesh_shape, cap, fields, outgoing, tracers, mask, height, flow, depth):
    planes, rows, cols = tracers.shape
    total = outgoing.shape[0]
    slots = cap * max(1, min(total, 128 // cap))
    rims = halo_shapes(5, rows, cols)
    lines = [(planes, cols), (planes, cols), (rows, LANES), (rows, LANES)]
    outs = rims + lines + [(fields, rows, cols), (4, rows, cols)]
    pieces = len(rims) + len(lines)
    scratch = (
        [outgoing.shape, (5, rows, cols)]
        + [(planes, rows, LANES)] * 2
        + [(planes, 8, cols)] * 2
        + lines
        + [(cols // LANES * fields * slots, LANES), (slots, LANES)]
    )
    dma = pltpu.SemaphoreType.DMA
    return pl.pallas_call(
        functools.partial(move_kernel, mesh_shape, cap),
        out_shape=[jax.ShapeDtypeStruct(s, f32) for s in outs],
        in_specs=[vmem(), pl.BlockSpec(memory_space=pl.ANY)] + [vmem()] * 4,
        out_specs=[vmem()] * len(outs),
        scratch_shapes=[pltpu.VMEM(s, f32) for s in scratch]
        + [dma, dma((4,)), dma((total,)), dma((total,)), dma((pieces,)), dma((pieces,))],
        compiler_params=pltpu.CompilerParams(
            collective_id=0, has_side_effects=True, vmem_limit_bytes=VMEM_LIMIT
        ),
        cost_estimate=pl.CostEstimate(
            flops=4_000_000_000, bytes_accessed=20_000_000, transcendentals=0
        ),
        name="move",
    )(outgoing, tracers, mask, height, flow, depth)


def exchange_kernel(mesh_shape, band, *refs):
    grid = Grid(mesh_shape)
    greet_near(grid)
    halo = Halo(grid, band, (), refs[:-2], *refs[-2:])
    halo.start()
    halo.wait()


def exchange(mesh_shape, band):
    shapes = halo_shapes(*band.shape)
    dma = pltpu.SemaphoreType.DMA
    return pl.pallas_call(
        functools.partial(exchange_kernel, mesh_shape),
        out_shape=[jax.ShapeDtypeStruct(s, f32) for s in shapes],
        in_specs=[vmem()],
        out_specs=[vmem()] * len(shapes),
        scratch_shapes=[dma((len(shapes),)), dma((len(shapes),))],
        compiler_params=pltpu.CompilerParams(
            collective_id=1, has_side_effects=True, vmem_limit_bytes=VMEM_LIMIT
        ),
        cost_estimate=pl.CostEstimate(flops=1000, bytes_accessed=5_000_000, transcendentals=0),
        name="exchange",
    )(band)


def tracer_kernel(
    levels,
    tracer_hbm,
    south_ref,
    north_ref,
    west_ref,
    east_ref,
    mask_south_ref,
    mask_north_ref,
    mask_ref,
    depth_ref,
    flow_ref,
    forcing_ref,
    out_ref,
    held,
    mask_held,
    ratio_ref,
    sems,
):
    planes = held.shape[0]
    rows, cols = mask_ref.shape
    steps = rows // 8
    i = pl.program_id(0)

    def chunk(step):
        at = pl.multiple_of(step * 8, 8)
        return pltpu.make_async_copy(
            tracer_hbm.at[:, pl.ds(at, 8), :], held.at[:, pl.ds(at + 8, 8), :], sems.at[step]
        )

    @pl.when(i == 0)
    def _():
        for s in range(steps):
            chunk(s).start()
        for p in range(planes):
            held[p, 7:8, :] = south_ref[p : p + 1, :]
            held[p, rows + 8 : rows + 9, :] = north_ref[p : p + 1, :]
        mask_held[0:8, :] = mask_south_ref[3]
        mask_held[8 : rows + 8, :] = mask_ref[...].astype(f32)
        mask_held[rows + 8 : rows + 16, :] = mask_north_ref[3]
        chunk(0).wait()

    @pl.when(i < steps - 1)
    def _():
        chunk(i + 1).wait()

    base = pl.multiple_of(i * 8, 8)
    here = pl.ds(base + 8, 8)
    lane = lax.broadcasted_iota(jnp.int32, (8, cols), 1) % LANES
    sub = lax.broadcasted_iota(jnp.int32, (8, cols), 0)
    at_first, at_last = lane == 0, lane == LANES - 1
    at_bottom, at_top = sub == 0, sub == 7
    west_edges = west_ref[pl.ds(base, 8), :]
    east_edges = east_ref[pl.ds(base, 8), :]
    pieces = cols // LANES

    def sides(q, below, above, p):
        parts = [q[:, c * LANES : (c + 1) * LANES] for c in range(pieces)]
        up = [pltpu.roll(a, 1, 1) for a in parts]
        down = [pltpu.roll(a, LANES - 1, 1) for a in parts]
        west_edge = jnp.broadcast_to(west_edges[:, p : p + 1], (8, LANES))
        east_edge = jnp.broadcast_to(east_edges[:, p : p + 1], (8, LANES))
        west = jnp.where(
            at_first, jnp.concatenate([west_edge] + up[:-1], 1), jnp.concatenate(up, 1)
        )
        east = jnp.where(
            at_last, jnp.concatenate(down[1:] + [east_edge], 1), jnp.concatenate(down, 1)
        )
        south = jnp.where(at_bottom, jnp.broadcast_to(below, q.shape), pltpu.roll(q, 1, 0))
        north = jnp.where(at_top, jnp.broadcast_to(above, q.shape), pltpu.roll(q, 7, 0))
        return east, west, north, south

    mask = mask_held[here, :]
    mask_e, mask_w, mask_n, mask_s = sides(
        mask, mask_held[pl.ds(base + 7, 1), :], mask_held[pl.ds(base + 16, 1), :], planes
    )
    inverse = 1.0 / depth_ref[...]
    u = flow_ref[0] * inverse
    v = flow_ref[1] * inverse
    ce = mask_e * (diffuse - advect * jnp.minimum(u, 0.0))
    cw = mask_w * (diffuse + advect * jnp.maximum(u, 0.0))
    cn = mask_n * (diffuse - advect * jnp.minimum(v, 0.0))
    cs = mask_s * (diffuse + advect * jnp.maximum(v, 0.0))
    c0 = 1.0 - (ce + cw + cn + cs)

    depths = np.arange(levels, dtype=np.float32)
    absorb = np.exp(-depths / np.float32(3)) - np.exp(-(depths + 1) / np.float32(3))
    fade = np.exp(-depths / np.float32(2))
    stir = 0.5 * forcing_ref[7] * forcing_ref[7]
    sun = 0.5 * forcing_ref[4]
    ratio = None
    last = [None, None]
    lower = None
    for k in range(levels):
        upper = 0.2 + stir * float(fade[k]) if k < levels - 1 else None
        pivot = 1.0
        if upper is not None:
            pivot = pivot + upper
        if lower is not None:
            pivot = pivot + lower + lower * ratio
        scale = 1.0 / pivot
        if upper is not None:
            ratio = -upper * scale
            ratio_ref[k] = ratio
        for t in range(2):
            p = t * levels + k
            q = held[p, here, :]
            qe, qw, qn, qs = sides(
                q, held[p, pl.ds(base + 7, 1), :], held[p, pl.ds(base + 16, 1), :], p
            )
            side = c0 * q + ce * qe + cw * qw + cn * qn + cs * qs
            if t == 0:
                side = side + sun * float(absorb[k])
                if k == 0:
                    side = side + 0.5 * forcing_ref[3]
            elif k == 0:
                side = side + (0.5 * forcing_ref[5] - 0.3 * forcing_ref[6])
            if lower is not None:
                side = side + lower * last[t]
            last[t] = side * scale
            out_ref[p] = last[t]
        lower = upper
    ocean = mask > 0.5
    for k in range(levels - 1, -1, -1):
        for t in range(2):
            p = t * levels + k
            if k < levels - 1:
                last[t] = out_ref[p] - ratio_ref[k] * last[t]
            out_ref[p] = jnp.where(ocean, last[t], held[p, here, :])


def tracer_step(
    levels, tracers, south, north, west, east, mask_south, mask_north, mask, depth, flow, forcing
):
    planes, rows, cols = tracers.shape

    def band(*lead):
        zeros = (0,) * len(lead)
        return pl.BlockSpec((*lead, 8, cols), lambda i: (*zeros, i, 0))

    def full(a):
        zeros = (0,) * a.ndim
        return pl.BlockSpec(a.shape, lambda i: zeros)

    return pl.pallas_call(
        functools.partial(tracer_kernel, levels),
        out_shape=jax.ShapeDtypeStruct(tracers.shape, f32),
        grid=(rows // 8,),
        in_specs=[
            pl.BlockSpec(memory_space=pl.ANY),
            full(south),
            full(north),
            full(west),
            full(east),
            full(mask_south),
            full(mask_north),
            full(mask),
            band(),
            band(2),
            band(forcing.shape[0]),
        ],
        out_specs=band(planes),
        scratch_shapes=[
            pltpu.VMEM((planes, rows + 16, cols), f32),
            pltpu.VMEM((rows + 16, cols), f32),
            pltpu.VMEM((levels, 8, cols), f32),
            pltpu.SemaphoreType.DMA((rows // 8,)),
        ],
        compiler_params=pltpu.CompilerParams(
            vmem_limit_bytes=VMEM_LIMIT, dimension_semantics=("arbitrary",)
        ),
        cost_estimate=pl.CostEstimate(
            flops=100_000_000, bytes_accessed=40_000_000, transcendentals=0
        ),
        name="tracer",
    )(tracers, south, north, west, east, mask_south, mask_north, mask, depth, flow, forcing)


def baro_kernel(
    height_ref,
    flow_ref,
    mask_ref,
    depth_ref,
    baro_ref,
    *refs,
):
    rows, cols = height_ref.shape
    height_out, flow_out = refs[-2:]

    def widen(k, tile, around):
        s, n, w, e, sw, se, nw, ne = [a[k] for a in around]
        low = jnp.concatenate([sw, s, se], 1)
        mid = jnp.concatenate([w, tile, e], 1)
        top = jnp.concatenate([nw, n, ne], 1)
        return jnp.concatenate([low, mid, top], 0)

    def still(k, tile):
        return widen(k, tile, refs[:8])

    def forced(k):
        return widen(k, baro_ref[k], refs[8:16])

    height = still(0, height_ref[...])
    along = still(1, flow_ref[0])
    across = still(2, flow_ref[1])
    mask = still(3, mask_ref[...].astype(f32))
    bottom = -0.5 * still(4, depth_ref[...])
    pressure, wind_x, wind_y, source = [forced(k) for k in range(4)]
    tall, wide = height.shape

    def slope_x(a):
        return pltpu.roll(a, wide - 1, 1) - pltpu.roll(a, 1, 1)

    def slope_y(a):
        return pltpu.roll(a, tall - 1, 0) - pltpu.roll(a, 1, 0)

    for _ in range(SUB):
        level = mask * (height + pressure)
        along = mask * (damping * along + (bottom * slope_x(level) + wind_x))
        across = mask * (damping * across + (bottom * slope_y(level) + wind_y))
        height = mask * (height - 0.5 * (slope_x(along) + slope_y(across)) + source)
    inner = (slice(RIM, RIM + rows), slice(LANES, LANES + cols))
    height_out[...] = height[inner]
    flow_out[0] = along[inner]
    flow_out[1] = across[inner]


def local(
    mesh_shape,
    atm_flux,
    margin_source,
    margin_cell,
    margin_weight,
    margin_tile,
    land_mask,
    sea_depth,
    sea_height,
    transport,
    tracers,
):
    levels = tracers.shape[1]
    tile_rows, tile_cols = sea_height.shape
    fields = atm_flux.shape[0]
    tiles = mesh_shape[0] * mesh_shape[1] * mesh_shape[2]
    cap = 2 * margin_source.shape[0] // tiles
    parts = 1

    outgoing = pack(
        margin_tile[:, 0], atm_flux, margin_source, margin_cell, margin_weight, tiles, cap, parts
    )

    flat = tracers.reshape(2 * levels, tile_rows, tile_cols)
    *rim, south, north, west, east, forcing, baro = move(
        mesh_shape,
        cap,
        fields,
        outgoing[0],
        flat,
        land_mask,
        sea_height,
        transport,
        sea_depth,
    )
    halo = exchange(mesh_shape, baro)
    new_tracers = tracer_step(
        levels,
        flat,
        south,
        north,
        west,
        east,
        rim[0],
        rim[1],
        land_mask,
        sea_depth,
        transport,
        forcing,
    )
    height, flow = pl.pallas_call(
        baro_kernel,
        out_shape=(
            jax.ShapeDtypeStruct(sea_height.shape, f32),
            jax.ShapeDtypeStruct(transport.shape, f32),
        ),
        in_specs=[vmem()] * (5 + 2 * len(WAYS)),
        out_specs=(vmem(), vmem()),
        compiler_params=pltpu.CompilerParams(vmem_limit_bytes=VMEM_LIMIT),
        cost_estimate=pl.CostEstimate(flops=10_000_000, bytes_accessed=8_000_000, transcendentals=0),
        name="baro",
    )(sea_height, transport, land_mask, sea_depth, baro, *rim, *halo)
    return (height, flow, new_tracers.reshape(tracers.shape))


def solution(mesh):
    in_specs = (
        P(None, AXES),
        P(AXES, None),
        P(AXES, None),
        P(AXES, None),
        P(AXES, None),
        P(("comp", "ty"), "tx"),
        P(("comp", "ty"), "tx"),
        P(("comp", "ty"), "tx"),
        P(None, ("comp", "ty"), "tx"),
        P(None, None, ("comp", "ty"), "tx"),
    )
    out_specs = (
        P(("comp", "ty"), "tx"),
        P(None, ("comp", "ty"), "tx"),
        P(None, None, ("comp", "ty"), "tx"),
    )
    body = functools.partial(local, tuple(mesh.shape[axis] for axis in AXES))
    return jax.shard_map(body, mesh=mesh, in_specs=in_specs, out_specs=out_specs, check_vma=False)
```

time: 177 us -> 121 us (0.68)
  the two profiles are of different devices: /device:TPU:19 before, /device:TPU:5 now
where the time goes in v3:
time: 121 us
  Pallas kernels  120 us (99%)
    pallas_call x1, Pallas kernels, move(): pl.pallas_call(functools.partial(move_kernel, mesh_shape, cap), out_shape...  79.9 us
    pallas_call x1, Pallas kernels, exchange(): pl.pallas_call(functools.partial(exchange_kernel, mesh_shape), out_shape=...  15.1 us
    pallas_call x1, Pallas kernels, tracer_step(): pl.pallas_call(functools.partial(tracer_kernel, levels), out_shape=jax.Sh...  14.4 us
    pallas_call x1, Pallas kernels, pack(): pl.pallas_call(functools.partial(pack_kernel, cap), out_shape=[jax.ShapeD...  5.92 us
    pallas_call x1, Pallas kernels, local(): pl.pallas_call(baro_kernel, out_shape=(jax.ShapeDtypeStruct(sea_height.sh...  4.75 us

profile of v3, /device:TPU:5, one launch (start us, length us, event | category | flops | bytes accessed | tf_op | source)
XLA Modules:
  0.0 120.7 jit_solution(14562018180490841542)
XLA Ops:
  0.6 5.9 %pack.1.outgoing = f32[32,144,128]{2,1,0:T(8,128)} custom-call(s32[256]{0:T(256)} %bitcast.6, f32[8,16384]{1,0:T(8,128)} %flux_ref.1, s32[256,128]{1,0:T(8,128)} %src_ref.1, s32[256,128]{1,0:T(8,128)} %cell_ref.1, f32[256,128]{1,0:T(8,128)} %weight_ref.1), custom_call_target="tpu_custom_call" | custom-call | flops 10000000 | bytes 4000000 | tf_op jit(solution)/shard_map/pack/pallas_call | solution.py:85
  6.5 79.9 %move.1 = (f32[5,8,1024]{2,1,0:T(8,128)}, f32[5,8,1024]{2,1,0:T(8,128)}, f32[5,64,128]{2,1,0:T(8,128)}, f32[5,64,128]{2,1,0:T(8,128)}, f32[5,8,128]{2,1,0:T(8,12...) custom-call(f32[32,144,128]{2,1,0:T(8,128)} %pack.1.outgoing, ...), custom_call_target="tpu_custom_call" | custom-call | flops 4000000000 | bytes 20000000 | tf_op jit(solution)/shard_map/move/pallas_call | solution.py:421
  86.4 15.1 %exchange.1 = (f32[4,8,1024]{2,1,0:T(8,128)}, f32[4,8,1024]{2,1,0:T(8,128)}, f32[4,64,128]{2,1,0:T(8,128)}, f32[4,64,128]{2,1,0:T(8,128)}, f32[4,8,128]{2,1,0:T(...) custom-call(f32[4,64,1024]{2,1,0:T(8,128)} %get-tuple-element.27.band.baro_ref), custom_call_target="tpu_custom_call" | custom-call | flops 1000 | bytes 5000000 | tf_op jit(solution)/shard_map/exchange/pallas_call | solution.py:449
  101.5 4.8 %baro.1 = (f32[64,1024]{1,0:T(8,128)}, f32[2,64,1024]{2,1,0:T(8,128)}) custom-call(f32[64,1024]{1,0:T(8,128)} %height_ref.3, f32[2,64,1024]{2,1,0:T(8,128)} %flow_ref.5, s32[64,1024]{1,0:T(8,128)} %mask_ref.5, f32[64,1024]{1,0:T(8,128)} %depth_ref.5, f32[4,64,1024]{2,1,0:T(8,128)} %get-tuple-element.27.band.baro_ref, ...), custom_call_target="tpu_custom_call" | custom-call | flops 10000000 | bytes 8000000 | tf_op jit(solution)/shard_map/baro/pallas_call | solution.py:741
  106.3 14.4 %tracer.1 = f32[32,64,1024]{2,1,0:T(8,128)} custom-call(f32[32,64,1024]{2,1,0:T(8,128)} %bitcast.4, f32[32,1024]{1,0:T(8,128)} %get-tuple-element.46.south_ref, f32[32,1024]{1,0:T(8,128)} %get-tuple-element.47.north_ref, f32[64,128]{1,0:T(8,128)} %get-tuple-element.48.west_ref, f32[64,128]{1,0:T(8,128)} %get-tuple-element.49.east_ref, ...), custom_call_target="tpu_custom_call" | custom-call | flops 100000000 | bytes 40000000 | tf_op jit(solution)/shard_map/tracer/pallas_call | solution.py:607

commit v4 on v3

--- a/solution.py
+++ b/solution.py
@@ -130,21 +130,6 @@
         return (at[0] * self.depth + at[1]) * self.nx + at[2]
 
 
-def greet_near(grid):
-    barrier = pltpu.get_barrier_semaphore()
-    near = jnp.int32(0)
-    for way in WAYS:
-        near = near + grid.inside(*way).astype(jnp.int32)
-
-        @pl.when(grid.inside(*way))
-        def _(way=way):
-            pl.semaphore_signal(
-                barrier, inc=1, device_id=grid.place(*way), device_id_type=pl.DeviceIdType.MESH
-            )
-
-    pl.semaphore_wait(barrier, near)
-
-
 class Halo:
     def __init__(self, grid, band, lines, outs, send_sems, recv_sems):
         rows, cols = band.shape[1:]
@@ -197,6 +182,59 @@
 
 def halo_shapes(count, rows, cols):
     return [(count, RIM if dy else rows, LANES if dx else cols) for dy, dx in WAYS]
+
+
+def advect_band(i, held, mask_held, depth_ref, flow_ref, west_ref, east_ref, moved_ref):
+    planes = held.shape[0]
+    cols = held.shape[2]
+    base = pl.multiple_of(i * 8, 8)
+    here = pl.ds(base + 8, 8)
+    lane = lax.broadcasted_iota(jnp.int32, (8, cols), 1) % LANES
+    sub = lax.broadcasted_iota(jnp.int32, (8, cols), 0)
+    at_first, at_last = lane == 0, lane == LANES - 1
+    at_bottom, at_top = sub == 0, sub == 7
+    west_edges = west_ref[pl.ds(base, 8), :]
+    east_edges = east_ref[pl.ds(base, 8), :]
+    pieces = cols // LANES
+
+    def sides(q, below, above, p):
+        parts = [q[:, c * LANES : (c + 1) * LANES] for c in range(pieces)]
+        up = [pltpu.roll(a, 1, 1) for a in parts]
+        down = [pltpu.roll(a, LANES - 1, 1) for a in parts]
+        west_edge = jnp.broadcast_to(west_edges[:, p : p + 1], (8, LANES))
+        east_edge = jnp.broadcast_to(east_edges[:, p : p + 1], (8, LANES))
+        west = jnp.where(
+            at_first, jnp.concatenate([west_edge] + up[:-1], 1), jnp.concatenate(up, 1)
+        )
+        east = jnp.where(
+            at_last, jnp.concatenate(down[1:] + [east_edge], 1), jnp.concatenate(down, 1)
+        )
+        south = jnp.where(at_bottom, jnp.broadcast_to(below, q.shape), pltpu.roll(q, 1, 0))
+        north = jnp.where(at_top, jnp.broadcast_to(above, q.shape), pltpu.roll(q, 7, 0))
+        return east, west, north, south
+
+    mask = mask_held[here, :]
+    mask_e, mask_w, mask_n, mask_s = sides(
+        mask, mask_held[pl.ds(base + 7, 1), :], mask_held[pl.ds(base + 16, 1), :], planes
+    )
+    near = pl.ds(base, 8)
+    inverse = 1.0 / depth_ref[near, :]
+    u = flow_ref[0, near, :] * inverse
+    v = flow_ref[1, near, :] * inverse
+    ce = mask_e * (diffuse - advect * jnp.minimum(u, 0.0))
+    cw = mask_w * (diffuse + advect * jnp.maximum(u, 0.0))
+    cn = mask_n * (diffuse - advect * jnp.minimum(v, 0.0))
+    cs = mask_s * (diffuse + advect * jnp.maximum(v, 0.0))
+    c0 = 1.0 - (ce + cw + cn + cs)
+
+    ocean = mask > 0.5
+    for p in range(planes):
+        q = held[p, here, :]
+        qe, qw, qn, qs = sides(
+            q, held[p, pl.ds(base + 7, 1), :], held[p, pl.ds(base + 16, 1), :], p
+        )
+        moved = c0 * q + ce * qe + cw * qw + cn * qn + cs * qs
+        moved_ref[p, near, :] = jnp.where(ocean, moved, q)
 
 
 def move_kernel(
@@ -213,14 +251,14 @@
     grid = Grid(mesh_shape)
     count = len(WAYS) + 4
     outs = refs[:count]
-    forcing_ref, baro_ref = refs[count : count + 2]
+    forcing_ref, baro_ref, moved_hbm = refs[count : count + 3]
+    baro_outs = refs[count + 3 : count + 3 + len(WAYS)]
     (
         arrived,
         band,
-        west_blk,
-        east_blk,
-        low_blk,
-        high_blk,
+        held,
+        mask_held,
+        moved,
         top,
         bottom,
         last,
@@ -233,9 +271,13 @@
         in_sems,
         send_sems,
         recv_sems,
-    ) = refs[count + 2 :]
+        late_send_sems,
+        late_recv_sems,
+        store_sems,
+    ) = refs[count + 3 + len(WAYS) :]
     fields, rows, cols = forcing_ref.shape
-    planes = west_blk.shape[0]
+    planes = held.shape[0]
+    bands = rows // 8
     width = arrived.shape[2]
     highs = cols // LANES
     lines = highs * fields
@@ -258,15 +300,12 @@
     own = pltpu.make_async_copy(outgoing.at[me], arrived.at[me], own_sem)
     own.start()
     loads = [
-        pltpu.make_async_copy(src, dst, load_sems.at[k])
-        for k, (src, dst) in enumerate(
-            (
-                (tracer_hbm.at[:, :, pl.ds(0, LANES)], west_blk),
-                (tracer_hbm.at[:, :, pl.ds(cols - LANES, LANES)], east_blk),
-                (tracer_hbm.at[:, pl.ds(0, 8), :], low_blk),
-                (tracer_hbm.at[:, pl.ds(rows - 8, 8), :], high_blk),
-            )
+        pltpu.make_async_copy(
+            tracer_hbm.at[:, pl.ds(8 * k, 8), :],
+            held.at[:, pl.ds(8 * k + 8, 8), :],
+            load_sems.at[k],
         )
+        for k in range(bands)
     ]
     for load in loads:
         load.start()
@@ -296,19 +335,16 @@
     for load in loads:
         load.wait()
     lane = lax.broadcasted_iota(jnp.int32, (rows, LANES), 1)
-    for src, dst, col, side in (
-        (west_blk, first, 0, 0),
-        (east_blk, last, LANES - 1, cols - LANES),
-    ):
+    for dst, col, side in ((first, 0, 0), (last, LANES - 1, cols - LANES)):
         edge = band[3, :, side : side + LANES][:, col : col + 1]
         values = jnp.where(lane == planes, jnp.broadcast_to(edge, (rows, LANES)), 0.0)
         for p in range(planes):
-            column = src[p, :, col : col + 1]
+            column = held[p, 8 : rows + 8, side : side + LANES][:, col : col + 1]
             values = jnp.where(lane == p, jnp.broadcast_to(column, (rows, LANES)), values)
         dst[...] = values
     for p in range(planes):
-        bottom[p : p + 1, :] = low_blk[p, 0:1, :]
-        top[p : p + 1, :] = high_blk[p, 7:8, :]
+        bottom[p : p + 1, :] = held[p, 8:9, :]
+        top[p : p + 1, :] = held[p, rows + 7 : rows + 8, :]
     halo = Halo(grid, band, (top, bottom, last, first), outs, send_sems, recv_sems)
     halo.start()
 
@@ -387,19 +423,50 @@
         lax.fori_loop(0, fields, field_step, 0)
         return carry
 
-    lax.fori_loop(0, total // owners, group_step, 0)
+    groups = total // owners
+    lax.fori_loop(0, groups // 2, group_step, 0)
+    halo.wait()
+    south_ref, north_ref, west_ref, east_ref = outs[len(WAYS) :]
+    for p in range(planes):
+        held[p, 7:8, :] = south_ref[p : p + 1, :]
+        held[p, rows + 8 : rows + 9, :] = north_ref[p : p + 1, :]
+    mask_held[0:8, :] = outs[0][3]
+    mask_held[8 : rows + 8, :] = band[3]
+    mask_held[rows + 8 : rows + 16, :] = outs[1][3]
+
+    def store(i):
+        at = pl.ds(pl.multiple_of(i * 8, 8), 8)
+        return pltpu.make_async_copy(
+            moved.at[:, at, :], moved_hbm.at[:, at, :], store_sems.at[i]
+        )
+
+    def advect_step(i, carry):
+        advect_band(i, held, mask_held, depth_ref, flow_ref, west_ref, east_ref, moved)
+        store(i).start()
+        return carry
+
+    lax.fori_loop(0, bands, advect_step, 0)
+    lax.fori_loop(groups // 2, groups, group_step, 0)
     baro_ref[0] = 0.5 * forcing_ref[2]
     baro_ref[1] = 0.5 * forcing_ref[0]
     baro_ref[2] = 0.5 * forcing_ref[1]
     baro_ref[3] = 0.1 * (forcing_ref[6] - forcing_ref[5])
 
-    halo.wait()
+    late = Halo(grid, baro_ref, (), baro_outs, late_send_sems, late_recv_sems)
+    late.start()
 
     def finish(d, carry):
         shift(d).wait_send()
         return carry
 
     lax.fori_loop(1, total, finish, 0)
+
+    def stored(i, carry):
+        store(i).wait()
+        return carry
+
+    lax.fori_loop(0, bands, stored, 0)
+    late.wait()
 
 
 def move(mesh_shape, cap, fields, outgoing, tracers, mask, height, flow, depth):
@@ -408,12 +475,15 @@
     slots = cap * max(1, min(total, 128 // cap))
     rims = halo_shapes(5, rows, cols)
     lines = [(planes, cols), (planes, cols), (rows, LANES), (rows, LANES)]
-    outs = rims + lines + [(fields, rows, cols), (4, rows, cols)]
+    outs = rims + lines + [(fields, rows, cols), (4, rows, cols), tracers.shape]
+    hbm = len(outs) - 1
+    outs = outs + halo_shapes(4, rows, cols)
+    places = [vmem()] * len(outs)
+    places[hbm] = pl.BlockSpec(memory_space=pl.ANY)
     pieces = len(rims) + len(lines)
     scratch = (
         [outgoing.shape, (5, rows, cols)]
-        + [(planes, rows, LANES)] * 2
-        + [(planes, 8, cols)] * 2
+        + [(planes, rows + 16, cols), (rows + 16, cols), tracers.shape]
         + lines
         + [(cols // LANES * fields * slots, LANES), (slots, LANES)]
     )
@@ -422,139 +492,33 @@
         functools.partial(move_kernel, mesh_shape, cap),
         out_shape=[jax.ShapeDtypeStruct(s, f32) for s in outs],
         in_specs=[vmem(), pl.BlockSpec(memory_space=pl.ANY)] + [vmem()] * 4,
-        out_specs=[vmem()] * len(outs),
+        out_specs=places,
         scratch_shapes=[pltpu.VMEM(s, f32) for s in scratch]
-        + [dma, dma((4,)), dma((total,)), dma((total,)), dma((pieces,)), dma((pieces,))],
+        + [dma, dma((rows // 8,)), dma((total,)), dma((total,)), dma((pieces,)), dma((pieces,))]
+        + [dma((len(WAYS),)), dma((len(WAYS),)), dma((rows // 8,))],
         compiler_params=pltpu.CompilerParams(
             collective_id=0, has_side_effects=True, vmem_limit_bytes=VMEM_LIMIT
         ),
         cost_estimate=pl.CostEstimate(
-            flops=4_000_000_000, bytes_accessed=20_000_000, transcendentals=0
+            flops=4_000_000_000, bytes_accessed=40_000_000, transcendentals=0
         ),
         name="move",
     )(outgoing, tracers, mask, height, flow, depth)
 
 
-def exchange_kernel(mesh_shape, band, *refs):
-    grid = Grid(mesh_shape)
-    greet_near(grid)
-    halo = Halo(grid, band, (), refs[:-2], *refs[-2:])
-    halo.start()
-    halo.wait()
-
-
-def exchange(mesh_shape, band):
-    shapes = halo_shapes(*band.shape)
-    dma = pltpu.SemaphoreType.DMA
-    return pl.pallas_call(
-        functools.partial(exchange_kernel, mesh_shape),
-        out_shape=[jax.ShapeDtypeStruct(s, f32) for s in shapes],
-        in_specs=[vmem()],
-        out_specs=[vmem()] * len(shapes),
-        scratch_shapes=[dma((len(shapes),)), dma((len(shapes),))],
-        compiler_params=pltpu.CompilerParams(
-            collective_id=1, has_side_effects=True, vmem_limit_bytes=VMEM_LIMIT
-        ),
-        cost_estimate=pl.CostEstimate(flops=1000, bytes_accessed=5_000_000, transcendentals=0),
-        name="exchange",
-    )(band)
-
-
-def tracer_kernel(
-    levels,
-    tracer_hbm,
-    south_ref,
-    north_ref,
-    west_ref,
-    east_ref,
-    mask_south_ref,
-    mask_north_ref,
-    mask_ref,
-    depth_ref,
-    flow_ref,
-    forcing_ref,
-    out_ref,
-    held,
-    mask_held,
-    ratio_ref,
-    sems,
-):
-    planes = held.shape[0]
-    rows, cols = mask_ref.shape
-    steps = rows // 8
-    i = pl.program_id(0)
-
-    def chunk(step):
-        at = pl.multiple_of(step * 8, 8)
-        return pltpu.make_async_copy(
-            tracer_hbm.at[:, pl.ds(at, 8), :], held.at[:, pl.ds(at + 8, 8), :], sems.at[step]
-        )
-
-    @pl.when(i == 0)
-    def _():
-        for s in range(steps):
-            chunk(s).start()
-        for p in range(planes):
-            held[p, 7:8, :] = south_ref[p : p + 1, :]
-            held[p, rows + 8 : rows + 9, :] = north_ref[p : p + 1, :]
-        mask_held[0:8, :] = mask_south_ref[3]
-        mask_held[8 : rows + 8, :] = mask_ref[...].astype(f32)
-        mask_held[rows + 8 : rows + 16, :] = mask_north_ref[3]
-        chunk(0).wait()
-
-    @pl.when(i < steps - 1)
-    def _():
-        chunk(i + 1).wait()
-
-    base = pl.multiple_of(i * 8, 8)
-    here = pl.ds(base + 8, 8)
-    lane = lax.broadcasted_iota(jnp.int32, (8, cols), 1) % LANES
-    sub = lax.broadcasted_iota(jnp.int32, (8, cols), 0)
-    at_first, at_last = lane == 0, lane == LANES - 1
-    at_bottom, at_top = sub == 0, sub == 7
-    west_edges = west_ref[pl.ds(base, 8), :]
-    east_edges = east_ref[pl.ds(base, 8), :]
-    pieces = cols // LANES
-
-    def sides(q, below, above, p):
-        parts = [q[:, c * LANES : (c + 1) * LANES] for c in range(pieces)]
-        up = [pltpu.roll(a, 1, 1) for a in parts]
-        down = [pltpu.roll(a, LANES - 1, 1) for a in parts]
-        west_edge = jnp.broadcast_to(west_edges[:, p : p + 1], (8, LANES))
-        east_edge = jnp.broadcast_to(east_edges[:, p : p + 1], (8, LANES))
-        west = jnp.where(
-            at_first, jnp.concatenate([west_edge] + up[:-1], 1), jnp.concatenate(up, 1)
-        )
-        east = jnp.where(
-            at_last, jnp.concatenate(down[1:] + [east_edge], 1), jnp.concatenate(down, 1)
-        )
-        south = jnp.where(at_bottom, jnp.broadcast_to(below, q.shape), pltpu.roll(q, 1, 0))
-        north = jnp.where(at_top, jnp.broadcast_to(above, q.shape), pltpu.roll(q, 7, 0))
-        return east, west, north, south
-
-    mask = mask_held[here, :]
-    mask_e, mask_w, mask_n, mask_s = sides(
-        mask, mask_held[pl.ds(base + 7, 1), :], mask_held[pl.ds(base + 16, 1), :], planes
-    )
-    inverse = 1.0 / depth_ref[...]
-    u = flow_ref[0] * inverse
-    v = flow_ref[1] * inverse
-    ce = mask_e * (diffuse - advect * jnp.minimum(u, 0.0))
-    cw = mask_w * (diffuse + advect * jnp.maximum(u, 0.0))
-    cn = mask_n * (diffuse - advect * jnp.minimum(v, 0.0))
-    cs = mask_s * (diffuse + advect * jnp.maximum(v, 0.0))
-    c0 = 1.0 - (ce + cw + cn + cs)
-
+def solve_kernel(levels, moved_ref, mask_ref, forcing_ref, out_ref, ratio_ref):
     depths = np.arange(levels, dtype=np.float32)
     absorb = np.exp(-depths / np.float32(3)) - np.exp(-(depths + 1) / np.float32(3))
     fade = np.exp(-depths / np.float32(2))
-    stir = 0.5 * forcing_ref[7] * forcing_ref[7]
-    sun = 0.5 * forcing_ref[4]
+    ocean = mask_ref[...].astype(f32)
+    floor = 0.2 * ocean
+    stir = (0.5 * ocean) * forcing_ref[7] * forcing_ref[7]
+    sun = (0.5 * ocean) * forcing_ref[4]
     ratio = None
     last = [None, None]
     lower = None
     for k in range(levels):
-        upper = 0.2 + stir * float(fade[k]) if k < levels - 1 else None
+        upper = floor + stir * float(fade[k]) if k < levels - 1 else None
         pivot = 1.0
         if upper is not None:
             pivot = pivot + upper
@@ -566,76 +530,48 @@
             ratio_ref[k] = ratio
         for t in range(2):
             p = t * levels + k
-            q = held[p, here, :]
-            qe, qw, qn, qs = sides(
-                q, held[p, pl.ds(base + 7, 1), :], held[p, pl.ds(base + 16, 1), :], p
-            )
-            side = c0 * q + ce * qe + cw * qw + cn * qn + cs * qs
+            side = moved_ref[p]
             if t == 0:
                 side = side + sun * float(absorb[k])
                 if k == 0:
-                    side = side + 0.5 * forcing_ref[3]
+                    side = side + (0.5 * ocean) * forcing_ref[3]
             elif k == 0:
-                side = side + (0.5 * forcing_ref[5] - 0.3 * forcing_ref[6])
+                side = side + ocean * (0.5 * forcing_ref[5] - 0.3 * forcing_ref[6])
             if lower is not None:
                 side = side + lower * last[t]
             last[t] = side * scale
             out_ref[p] = last[t]
         lower = upper
-    ocean = mask > 0.5
-    for k in range(levels - 1, -1, -1):
+    for k in range(levels - 2, -1, -1):
         for t in range(2):
             p = t * levels + k
-            if k < levels - 1:
-                last[t] = out_ref[p] - ratio_ref[k] * last[t]
-            out_ref[p] = jnp.where(ocean, last[t], held[p, here, :])
-
-
-def tracer_step(
-    levels, tracers, south, north, west, east, mask_south, mask_north, mask, depth, flow, forcing
-):
-    planes, rows, cols = tracers.shape
+            last[t] = out_ref[p] - ratio_ref[k] * last[t]
+            out_ref[p] = last[t]
+
+
+def solve_step(levels, moved, mask, forcing):
+    planes, rows, cols = moved.shape
+    tall = 16 if rows % 16 == 0 else 8
 
     def band(*lead):
         zeros = (0,) * len(lead)
-        return pl.BlockSpec((*lead, 8, cols), lambda i: (*zeros, i, 0))
-
-    def full(a):
-        zeros = (0,) * a.ndim
-        return pl.BlockSpec(a.shape, lambda i: zeros)
+        return pl.BlockSpec((*lead, tall, cols), lambda i: (*zeros, i, 0))
 
     return pl.pallas_call(
-        functools.partial(tracer_kernel, levels),
-        out_shape=jax.ShapeDtypeStruct(tracers.shape, f32),
-        grid=(rows // 8,),
-        in_specs=[
-            pl.BlockSpec(memory_space=pl.ANY),
-            full(south),
-            full(north),
-            full(west),
-            full(east),
-            full(mask_south),
-            full(mask_north),
-            full(mask),
-            band(),
-            band(2),
-            band(forcing.shape[0]),
-        ],
+        functools.partial(solve_kernel, levels),
+        out_shape=jax.ShapeDtypeStruct(moved.shape, f32),
+        grid=(rows // tall,),
+        in_specs=[band(planes), band(), band(forcing.shape[0])],
         out_specs=band(planes),
-        scratch_shapes=[
-            pltpu.VMEM((planes, rows + 16, cols), f32),
-            pltpu.VMEM((rows + 16, cols), f32),
-            pltpu.VMEM((levels, 8, cols), f32),
-            pltpu.SemaphoreType.DMA((rows // 8,)),
-        ],
+        scratch_shapes=[pltpu.VMEM((levels, tall, cols), f32)],
         compiler_params=pltpu.CompilerParams(
             vmem_limit_bytes=VMEM_LIMIT, dimension_semantics=("arbitrary",)
         ),
         cost_estimate=pl.CostEstimate(
-            flops=100_000_000, bytes_accessed=40_000_000, transcendentals=0
+            flops=30_000_000, bytes_accessed=25_000_000, transcendentals=0
         ),
-        name="tracer",
-    )(tracers, south, north, west, east, mask_south, mask_north, mask, depth, flow, forcing)
+        name="solve",
+    )(moved, mask, forcing)
 
 
 def baro_kernel(
@@ -712,7 +648,7 @@
     )
 
     flat = tracers.reshape(2 * levels, tile_rows, tile_cols)
-    *rim, south, north, west, east, forcing, baro = move(
+    found = move(
         mesh_shape,
         cap,
         fields,
@@ -723,21 +659,10 @@
         transport,
         sea_depth,
     )
-    halo = exchange(mesh_shape, baro)
-    new_tracers = tracer_step(
-        levels,
-        flat,
-        south,
-        north,
-        west,
-        east,
-        rim[0],
-        rim[1],
-        land_mask,
-        sea_depth,
-        transport,
-        forcing,
-    )
+    ways = len(WAYS)
+    rim, halo = found[:ways], found[-ways:]
+    forcing, baro, moved = found[-ways - 3 : -ways]
+    new_tracers = solve_step(levels, moved, land_mask, forcing)
     height, flow = pl.pallas_call(
         baro_kernel,
         out_shape=(

time: 121 us -> 135 us (1.12)
  the two profiles are of different devices: /device:TPU:5 before, /device:TPU:0 now
where the time goes in v4:
time: 135 us
  Pallas kernels  134 us (99%)
    pallas_call x1, Pallas kernels, move(): pl.pallas_call(functools.partial(move_kernel, mesh_shape, cap), out_shape...  115 us
    pallas_call x1, Pallas kernels, solve_step(): pl.pallas_call(functools.partial(solve_kernel, levels), out_shape=jax.Sha...  9.16 us
    pallas_call x1, Pallas kernels, pack(): pl.pallas_call(functools.partial(pack_kernel, cap), out_shape=[jax.ShapeD...  5.92 us
    pallas_call x1, Pallas kernels, local(): pl.pallas_call(baro_kernel, out_shape=(jax.ShapeDtypeStruct(sea_height.sh...  4.75 us

profile of v4, /device:TPU:0, one launch (start us, length us, event | category | flops | bytes accessed | tf_op | source)
XLA Modules:
  0.0 135.1 jit_solution(9810700259088562151)
XLA Ops:
  0.6 5.9 %pack.1.outgoing = f32[32,144,128]{2,1,0:T(8,128)} custom-call(s32[256]{0:T(256)} %bitcast.4, f32[8,16384]{1,0:T(8,128)} %flux_ref.1, s32[256,128]{1,0:T(8,128)} %src_ref.1, s32[256,128]{1,0:T(8,128)} %cell_ref.1, f32[256,128]{1,0:T(8,128)} %weight_ref.1), custom_call_target="tpu_custom_call" | custom-call | flops 10000000 | bytes 4000000 | tf_op jit(solution)/shard_map/pack/pallas_call | solution.py:85
  6.5 114.6 %move.1 = (f32[5,8,1024]{2,1,0:T(8,128)}, f32[5,8,1024]{2,1,0:T(8,128)}, f32[5,64,128]{2,1,0:T(8,128)}, f32[5,64,128]{2,1,0:T(8,128)}, f32[5,8,128]{2,1,0:T(8,12...) custom-call(f32[32,144,128]{2,1,0:T(8,128)} %pack.1.outgoing, ...), custom_call_target="tpu_custom_call" | custom-call | flops 4000000000 | bytes 40000000 | tf_op jit(solution)/shard_map/move/pallas_call | solution.py:491
  121.1 4.8 %baro.1 = (f32[64,1024]{1,0:T(8,128)}, f32[2,64,1024]{2,1,0:T(8,128)}) custom-call(f32[64,1024]{1,0:T(8,128)} %height_ref.3, f32[2,64,1024]{2,1,0:T(8,128)} %flow_ref.3, s32[64,1024]{1,0:T(8,128)} %mask_ref.5, f32[64,1024]{1,0:T(8,128)} %depth_ref.3, f32[4,64,1024]{2,1,0:T(8,128)} %get-tuple-element.24.baro_ref, f32[5,8,1024]{2,1,0:T(8,128)} %get-tuple-element.25.refs_0_, ...), custom_call_target="tpu_custom_call" | custom-call | flops 10000000 | bytes 8000000 | tf_op jit(solution)/shard_map/baro/pallas_call | solution.py:666
  125.9 9.2 %solve.1 = f32[32,64,1024]{2,1,0:T(8,128)} custom-call(f32[32,64,1024]{2,1,0:T(8,128)} %get-tuple-element.43.moved_ref, s32[64,1024]{1,0:T(8,128)} %mask_ref.5, f32[8,64,1024]{2,1,0:T(8,128)} %get-tuple-element.44.forcing_ref), custom_call_target="tpu_custom_call" | custom-call | flops 30000000 | bytes 25000000 | tf_op jit(solution)/shard_map/solve/pallas_call | solution.py:560

commit v5 on v4

--- a/solution.py
+++ b/solution.py
@@ -325,7 +325,8 @@
         shift(d).start()
         return carry
 
-    lax.fori_loop(1, total, start, 0)
+    early = min(total, grid.comps * grid.depth)
+    lax.fori_loop(1, early, start, 0)
 
     band[0] = height_ref[...]
     band[1] = flow_ref[0]
@@ -347,6 +348,7 @@
         top[p : p + 1, :] = held[p, rows + 7 : rows + 8, :]
     halo = Halo(grid, band, (top, bottom, last, first), outs, send_sems, recv_sems)
     halo.start()
+    lax.fori_loop(early, total, start, 0)
 
     forcing_ref[...] = jnp.zeros(forcing_ref.shape, f32)
     low_iota = lax.broadcasted_iota(jnp.int32, (LANES, width), 0)

time: 135 us -> 129 us (0.956)
  the two profiles are of different devices: /device:TPU:0 before, /device:TPU:5 now
where the time goes in v5:
time: 129 us
  Pallas kernels  128 us (99%)
    pallas_call x1, Pallas kernels, move(): pl.pallas_call(functools.partial(move_kernel, mesh_shape, cap), out_shape...  108 us
    pallas_call x1, Pallas kernels, solve_step(): pl.pallas_call(functools.partial(solve_kernel, levels), out_shape=jax.Sha...  9.16 us
    pallas_call x1, Pallas kernels, pack(): pl.pallas_call(functools.partial(pack_kernel, cap), out_shape=[jax.ShapeD...  5.92 us
    pallas_call x1, Pallas kernels, local(): pl.pallas_call(baro_kernel, out_shape=(jax.ShapeDtypeStruct(sea_height.sh...  4.75 us

profile of v5, /device:TPU:5, one launch (start us, length us, event | category | flops | bytes accessed | tf_op | source)
XLA Modules:
  0.0 128.9 jit_solution(12752574970400923498)
XLA Ops:
  0.6 5.9 %pack.1.outgoing = f32[32,144,128]{2,1,0:T(8,128)} custom-call(s32[256]{0:T(256)} %bitcast.4, f32[8,16384]{1,0:T(8,128)} %flux_ref.1, s32[256,128]{1,0:T(8,128)} %src_ref.1, s32[256,128]{1,0:T(8,128)} %cell_ref.1, f32[256,128]{1,0:T(8,128)} %weight_ref.1), custom_call_target="tpu_custom_call" | custom-call | flops 10000000 | bytes 4000000 | tf_op jit(solution)/shard_map/pack/pallas_call | solution.py:85
  6.5 108.4 %move.1 = (f32[5,8,1024]{2,1,0:T(8,128)}, f32[5,8,1024]{2,1,0:T(8,128)}, f32[5,64,128]{2,1,0:T(8,128)}, f32[5,64,128]{2,1,0:T(8,128)}, f32[5,8,128]{2,1,0:T(8,12...) custom-call(f32[32,144,128]{2,1,0:T(8,128)} %pack.1.outgoing, ...), custom_call_target="tpu_custom_call" | custom-call | flops 4000000000 | bytes 40000000 | tf_op jit(solution)/shard_map/move/pallas_call | solution.py:493
  115.0 4.8 %baro.1 = (f32[64,1024]{1,0:T(8,128)}, f32[2,64,1024]{2,1,0:T(8,128)}) custom-call(f32[64,1024]{1,0:T(8,128)} %height_ref.3, f32[2,64,1024]{2,1,0:T(8,128)} %flow_ref.3, s32[64,1024]{1,0:T(8,128)} %mask_ref.5, f32[64,1024]{1,0:T(8,128)} %depth_ref.3, f32[4,64,1024]{2,1,0:T(8,128)} %get-tuple-element.24.baro_ref, f32[5,8,1024]{2,1,0:T(8,128)} %get-tuple-element.25.refs_0_, ...), custom_call_target="tpu_custom_call" | custom-call | flops 10000000 | bytes 8000000 | tf_op jit(solution)/shard_map/baro/pallas_call | solution.py:668
  119.7 9.2 %solve.1 = f32[32,64,1024]{2,1,0:T(8,128)} custom-call(f32[32,64,1024]{2,1,0:T(8,128)} %get-tuple-element.43.moved_ref, s32[64,1024]{1,0:T(8,128)} %mask_ref.5, f32[8,64,1024]{2,1,0:T(8,128)} %get-tuple-element.44.forcing_ref), custom_call_target="tpu_custom_call" | custom-call | flops 30000000 | bytes 25000000 | tf_op jit(solution)/shard_map/solve/pallas_call | solution.py:562
